TPU v7x, 32 devices: a whole 2x2x4 slice. The times are simulated.
32 devices in a mesh: group: 8 (over z, y), tensor: 4 (over x, core).
Axes of the slice: x: 2, y: 2, z: 4, core: 2. Of those that a mesh axis runs over, the one named last changes fastest.
Arguments:
- tokens: bfloat16 [16, 128, 4608], P('group', None, 'tensor'), may hold values from -6 to 6
- targets: bfloat16 [16, 128, 4608], P('group', None, 'tensor'), may hold values from -6 to 6
- token_counts: int32 [16], P('group'), may hold values from 1 to 128, as said below
- sample_counts: int32 [16], replicated, may hold values from 1 to 1000
- up_weight: bfloat16 [6912, 4608], P('tensor'), may hold values from -0.09375 to 0.09375
- down_weight: bfloat16 [6912, 4608], P('tensor'), may hold values from -0.078125 to 0.078125
- momentum_up: float32 [6912, 4608], P('tensor', 'group'), may hold values from -6 to 6
- momentum_down: float32 [6912, 4608], P('tensor', 'group'), may hold values from -6 to 6
Outputs:
- new_momentum_up: float32 [6912, 4608], P('tensor', 'group')
- new_momentum_down: float32 [6912, 4608], P('tensor', 'group')
Inputs may be any that keep to these rules, and one draw needn't show every extreme that they name: `token_counts`: some client has exactly 128 valid rows and some exactly 1.
All inputs are finite; a program needn't handle non-finite values.
Results may differ from a plain program's by a relative error of at most 0.02.
Values may be sent and summed in bfloat16 or wider, within the bound.
A program may use at most 384 MiB of HBM per device.

v0:
```python
import jax
import jax.numpy as jnp
from jax import lax
from jax.sharding import PartitionSpec as P

STEPS = 2


client_rate = 0.0003
momentum_decay = 0.9


def silu_slope(preact):
    logistic = jax.nn.sigmoid(preact)
    return logistic * (1.0 + preact * (1.0 - logistic))


def contract_rows(former, latter):
    return lax.dot_general(
        former, latter, (((0,), (0,)), ((), ())), preferred_element_type=jnp.float32
    )


def contract_cols(former, latter):
    return lax.dot_general(
        former, latter, (((1,), (1,)), ((), ())), preferred_element_type=jnp.float32
    )


def backward(inputs, hidden, preact, residual, weight_down):
    grad_down = contract_rows(hidden, residual)
    slopes = (contract_cols(residual, weight_down) * silu_slope(preact)).astype(jnp.bfloat16)
    grad_up = contract_rows(slopes, inputs)
    return (grad_up, grad_down)


def local_pass(inputs, target, row_mask, weight_up, weight_down):
    preact = contract_cols(inputs, weight_up)
    hidden = jax.nn.silu(preact).astype(jnp.bfloat16)
    partial_out = jnp.dot(hidden, weight_down, preferred_element_type=jnp.float32)
    own_cols = lax.psum_scatter(
        partial_out.astype(jnp.bfloat16), "tensor", scatter_dimension=1, tiled=True
    ).astype(jnp.float32)
    residual = (row_mask * (own_cols - target.astype(jnp.float32))).astype(jnp.bfloat16)
    residual = lax.all_gather(residual, "tensor", axis=1, tiled=True)
    return backward(inputs, hidden, preact, residual, weight_down)


def on_device(
    tokens, targets, token_counts, sample_counts, up_weight, down_weight, momentum_up, momentum_down
):
    gathered = lax.all_gather(tokens, "tensor", axis=2, tiled=True)
    slot_count, row_count = (gathered.shape[0], gathered.shape[1])
    positions = jnp.arange(row_count, dtype=jnp.int32)[:, None]
    first_client = lax.axis_index("group") * slot_count
    client_weights = lax.dynamic_slice_in_dim(sample_counts, first_client, slot_count).astype(
        jnp.float32
    )
    row_masks = [
        (positions < token_counts[slot_num]).astype(jnp.float32) for slot_num in range(slot_count)
    ]
    acc_up = jnp.zeros(up_weight.shape, jnp.float32)
    acc_down = jnp.zeros(down_weight.shape, jnp.float32)
    for slot_num in range(slot_count):
        weight_up, weight_down = (up_weight, down_weight)
        for local_step in range(STEPS):
            if local_step > 0:
                grad_up, grad_down = local_pass(
                    gathered[slot_num],
                    targets[slot_num],
                    row_masks[slot_num],
                    weight_up,
                    weight_down,
                )
            else:
                grad_up, grad_down = local_pass(
                    gathered[slot_num],
                    targets[slot_num],
                    row_masks[slot_num],
                    weight_up,
                    weight_down,
                )
            acc_up = acc_up + client_weights[slot_num] * grad_up
            acc_down = acc_down + client_weights[slot_num] * grad_down
            if local_step + 1 < STEPS:
                weight_up = (weight_up.astype(jnp.float32) - client_rate * grad_up).astype(
                    jnp.bfloat16
                )
                weight_down = (weight_down.astype(jnp.float32) - client_rate * grad_down).astype(
                    jnp.bfloat16
                )
    group_up = acc_up.astype(jnp.bfloat16)
    group_down = acc_down.astype(jnp.bfloat16)
    sum_up, sum_down = (
        lax.psum_scatter(group_up, "group", scatter_dimension=1, tiled=True).astype(jnp.float32),
        lax.psum_scatter(group_down, "group", scatter_dimension=1, tiled=True).astype(jnp.float32),
    )
    weight_total = jnp.sum(sample_counts).astype(jnp.float32)
    new_momentum_up = momentum_decay * momentum_up + sum_up / weight_total
    new_momentum_down = momentum_decay * momentum_down + sum_down / weight_total
    return (new_momentum_up, new_momentum_down)


def solution(mesh):
    placed = (
        P("group", None, "tensor"),
        P("group", None, "tensor"),
        P("group"),
        P(),
        P("tensor", None),
        P("tensor", None),
        P("tensor", "group"),
        P("tensor", "group"),
    )
    return jax.shard_map(
        on_device,
        mesh=mesh,
        in_specs=placed,
        out_specs=(P("tensor", "group"), P("tensor", "group")),
        check_vma=False,
    )
```

profile of v0, /device:TPU:10, one launch (start us, length us, event | category | flops | bytes accessed | tf_op | source)
XLA Modules:
  0.0 992.0 jit_solution(7276309482160924434)
XLA Ops:
  7.9 25.9 %all-gather.6.cloned.1.call-done = bf16[2,128,4608]{2,1,0:T(8,128)(2,1)} async-done(((bf16[2,128,1152]{2,1,0:T(8,128)(2,1)}), bf16[2,128,4608]{2,1,0:T(8,128)(2,1)}) %all-gather.6.cloned.1.call-update) | async-done | bytes 2359312 | tf_op jit(solution)/shard_map/all_gather | solution.py:52
  33.9 8.2 fusion.39
  44.3 3.7 convolution_convert_fusion.3
  50.4 7.8 fusion.40
  59.1 9.3 convolution_convert_fusion.1
  77.4 27.9 %reduce-scatter.23.cloned.1.call-done = bf16[1152,128]{1,0:T(8,128)(2,1)} async-done(((bf16[4608,128]{1,0:T(8,128)(2,1)}), bf16[1152,128]{1,0:T(8,128)(2,1)}) %reduce-scatter.23.cloned.1.call-update) | async-done | bytes 294928
  110.4 16.5 %all-gather.12.cloned.1.call-done = bf16[128,4608]{1,0:T(8,128)(2,1)} async-done(((bf16[128,1152]{1,0:T(8,128)(2,1)}), bf16[128,4608]{1,0:T(8,128)(2,1)}) %all-gather.12.cloned.1.call-update) | async-done | bytes 1179664 | tf_op jit(solution)/shard_map/all_gather | solution.py:45
  126.9 25.8 %fusion.24 = f32[1728,4608]{1,0:T(8,128)} fusion(bf16[128,4608]{1,0:T(8,128)(2,1)} %all-gather.12.cloned.1.call-done, bf16[1728,4608]{1,0:T(8,128)(2,1)} %param.13, f32[128,1728]{0,1:T(8,128)} %copy-done.3, bf16[2,128,4608]{2,1,0:T(8,128)(2,1)S(1)} %copy-done.1), kind=kOutput, calls=%fused_computation.34 | convolution fusion | flops 4078854144 | bytes 51019776 | tf_op jit(solution)/shard_map/dot_general | solution.py:19
  152.7 16.4 %fusion.61 = f32[1728,4608]{1,0:T(8,128)} fusion(bf16[128,4608]{1,0:T(8,128)(2,1)} %all-gather.12.cloned.1.call-done, f32[128,1728]{0,1:T(8,128)} %copy-done.3), kind=kOutput, calls=%fused_computation.88 | convolution fusion | flops 2039537664 | bytes 33914880 | tf_op jit(solution)/shard_map/dot_general | solution.py:19
  169.1 17.8 %fusion.17 = f32[128,1728]{0,1:T(8,128)} fusion(bf16[1728,4608]{1,0:T(8,128)(2,1)} %param.12, f32[1728,4608]{1,0:T(8,128)} %fusion.24, bf16[2,128,4608]{2,1,0:T(8,128)(2,1)S(1)} %copy-done.1), kind=kOutput, calls=%fused_computation.29 | convolution fusion | flops 2070282240 | bytes 49840128 | tf_op jit(solution)/shard_map/dot_general | solution.py:25
  186.9 18.7 %convolution_convert_fusion = bf16[128,4608]{1,0:T(8,128)(2,1)} fusion(f32[128,1728]{0,1:T(8,128)} %fusion.17, bf16[1728,4608]{1,0:T(8,128)(2,1)} %param.13, f32[1728,4608]{1,0:T(8,128)} %fusion.61), kind=kOutput, calls=%fused_computation.18 | convolution fusion | flops 2071977984 | bytes 49840128 | tf_op jit(solution)/shard_map/dot_general | solution.py:40
  208.0 25.7 %fusion.26 = f32[1728,4608]{1,0:T(8,128)} fusion(bf16[128,4608]{1,0:T(8,128)(2,1)} %all-gather.8.cloned.1.call-done, bf16[1728,4608]{1,0:T(8,128)(2,1)} %param.13, f32[128,1728]{0,1:T(8,128)S(1)} %fusion.39, bf16[2,128,4608]{2,1,0:T(8,128)(2,1)S(1)} %copy-done.1), kind=kOutput, calls=%fused_computation.36 | convolution fusion | flops 4078854144 | bytes 51019776 | tf_op jit(solution)/shard_map/dot_general | solution.py:19
  233.7 16.8 %fusion.14 = f32[128,1728]{0,1:T(8,128)S(1)} fusion(bf16[1728,4608]{1,0:T(8,128)(2,1)} %param.12, f32[1728,4608]{1,0:T(8,128)} %fusion.26, bf16[2,128,4608]{2,1,0:T(8,128)(2,1)S(1)} %copy-done.1), kind=kOutput, calls=%fused_computation.28 | convolution fusion | flops 2070282240 | bytes 49840128 | tf_op jit(solution)/shard_map/dot_general | solution.py:25
  250.5 16.4 %fusion.59 = f32[1728,4608]{1,0:T(8,128)} fusion(bf16[128,4608]{1,0:T(8,128)(2,1)} %all-gather.8.cloned.1.call-done, f32[128,1728]{0,1:T(8,128)} %copy-done.2), kind=kOutput, calls=%fused_computation.86 | convolution fusion | flops 2039537664 | bytes 33914880 | tf_op jit(solution)/shard_map/dot_general | solution.py:19
  266.9 18.6 %convolution_convert_fusion.2 = bf16[128,4608]{1,0:T(8,128)(2,1)} fusion(f32[128,1728]{0,1:T(8,128)S(1)} %fusion.14, bf16[1728,4608]{1,0:T(8,128)(2,1)} %param.13, f32[1728,4608]{1,0:T(8,128)} %fusion.59), kind=kOutput, calls=%fused_computation.20 | convolution fusion | flops 2071977984 | bytes 49840128 | tf_op jit(solution)/shard_map/dot_general | solution.py:40
  289.2 24.6 %reduce-scatter.21.cloned.1.call-done = bf16[1152,128]{1,0:T(8,128)(2,1)} async-done(((bf16[4608,128]{1,0:T(8,128)(2,1)}), bf16[1152,128]{1,0:T(8,128)(2,1)}) %reduce-scatter.21.cloned.1.call-update) | async-done | bytes 294928
  319.3 16.2 %all-gather.10.cloned.1.call-done = bf16[128,4608]{1,0:T(8,128)(2,1)} async-done(((bf16[128,1152]{1,0:T(8,128)(2,1)}), bf16[128,4608]{1,0:T(8,128)(2,1)}) %all-gather.10.cloned.1.call-update) | async-done | bytes 1179664 | tf_op jit(solution)/shard_map/all_gather | solution.py:45
  335.4 14.1 %fusion.60 = f32[1728,4608]{1,0:T(8,128)} fusion(bf16[128,4608]{1,0:T(8,128)(2,1)} %all-gather.10.cloned.1.call-done, f32[128,1728]{0,1:T(8,128)S(1)} %fusion.14), kind=kOutput, calls=%fused_computation.87 | convolution fusion | flops 2039537664 | bytes 33914880 | tf_op jit(solution)/shard_map/dot_general | solution.py:19
  349.6 5.5 all-gather.14.cloned.1.call-done
  355.1 37.9 %fusion.5 = bf16[1728,4608]{1,0:T(8,128)(2,1)} fusion(f32[1728,4608]{1,0:T(8,128)} %fusion.59, f32[1728,4608]{1,0:T(8,128)} %fusion.60, f32[1728,4608]{1,0:T(8,128)} %fusion.61, bf16[128,4608]{1,0:T(8,128)(2,1)} %all-gather.14.cloned.1.call-done, f32[]{:T(128)} %bitcast.6, f32[]{:T(128)} %bitcast.5, f32[128,1728]{0,1:T(8,128)} %fusion.17), kind=kOutput, calls=%fused_computation.10 | convolution fusion | flops 2095276032 | bytes 113541128 | tf_op jit(solution)/shard_map/dot_general | solution.py:19
  393.0 20.3 %copy.40 = bf16[1728,4608]{0,1:T(8,128)(2,1)} copy(bf16[1728,4608]{1,0:T(8,128)(2,1)} %fusion.5) | data formatting | bytes 31850496
  413.4 31.2 %fusion.25 = f32[1728,4608]{1,0:T(8,128)} fusion(bf16[128,4608]{1,0:T(8,128)(2,1)} %all-gather.10.cloned.1.call-done, f32[128,1728]{0,1:T(8,128)S(1)} %fusion.14, bf16[2,128,4608]{2,1,0:T(8,128)(2,1)S(1)} %copy-done.1, bf16[1728,4608]{1,0:T(8,128)(2,1)} %param.13, f32[1728,4608]{1,0:T(8,128)} %fusion.59), kind=kOutput, calls=%fused_computation.35 | convolution fusion | flops 4110704640 | bytes 82870272 | tf_op jit(solution)/shard_map/dot_general | solution.py:19
  444.6 55.0 %fusion.7 = bf16[1728,4608]{1,0:T(8,128)(2,1)} fusion(f32[1728,4608]{1,0:T(8,128)} %fusion.26, f32[1728,4608]{1,0:T(8,128)} %fusion.25, f32[1728,4608]{1,0:T(8,128)} %fusion.24, f32[]{:T(128)} %bitcast.6, f32[]{:T(128)} %bitcast.5, bf16[2,128,4608]{2,1,0:T(8,128)(2,1)S(1)} %copy-done.1, bf16[128,4608]{1,0:T(8,128)(2,1)} %all-gather.14.cloned.1.call-done, ...), kind=kOutput, calls=%fused_computation.13 | convolution fusion | flops 4166443008 | bytes 162496512 | tf_op jit(solution)/shard_map/dot_general | solution.py:19
  499.6 20.3 %copy.38 = bf16[1728,4608]{0,1:T(8,128)(2,1)} copy(bf16[1728,4608]{1,0:T(8,128)(2,1)} %fusion.7) | data formatting | bytes 31850496
  521.8 5.8 copy.21
  527.6 5.6 copy.18
  533.2 157.4 %reduce-scatter.29.cloned.1.call-done = bf16[576,1728]{1,0:T(8,128)(2,1)} async-done(((bf16[4608,1728]{1,0:T(8,128)(2,1)}), bf16[576,1728]{1,0:T(8,128)(2,1)}) %reduce-scatter.29.cloned.1.call-update) | async-done | bytes 1990672
  694.1 4.9 divide_add_fusion
  699.1 5.6 copy.25
  704.6 266.6 %reduce-scatter.27.cloned.1.call-done = bf16[576,1728]{1,0:T(8,128)(2,1)} async-done(((bf16[4608,1728]{1,0:T(8,128)(2,1)}), bf16[576,1728]{1,0:T(8,128)(2,1)}) %reduce-scatter.27.cloned.1.call-update) | async-done | bytes 1990672
  974.7 4.8 divide_add_fusion.1
  979.5 5.5 copy.24
  (56 shorter events, 40.1 us)
Async XLA Ops:
  7.2 26.7 %all-gather.6.cloned.1.call-start = ((), (), s32[]{:S(2)}) async-start(), calls=%async_computation.6 | async-start | bytes 2949120 | tf_op jit(solution)/shard_map/all_gather | solution.py:52
  7.9 68.3 %reduce-scatter.19.cloned.1.call-start = ((), (), s32[]{:S(2)}) async-start(), calls=%async_computation.11 | async-start | bytes 1474560
  33.9 10.4 %copy-start = (bf16[1728,4608]{1,0:T(8,128)(2,1)S(1)}, bf16[1728,4608]{1,0:T(8,128)(2,1)}, u32[]{:S(2)}) copy-start(bf16[1728,4608]{1,0:T(8,128)(2,1)} %param.13) | copy-start | bytes 47775748
  44.3 163.8 %copy-start.2 = (f32[128,1728]{0,1:T(8,128)}, f32[128,1728]{0,1:T(8,128)S(1)}, u32[]{:S(2)}) copy-start(f32[128,1728]{0,1:T(8,128)S(1)} %fusion.39) | copy-start | bytes 2654212
  44.3 6.1 copy-start.1
  50.3 55.0 %reduce-scatter.23.cloned.1.call-start = ((), (), s32[]{:S(2)}) async-start(), calls=%async_computation.13 | async-start | bytes 1474560
  58.2 1.0 copy-start.3
  59.1 11.7 %copy-start.4 = (s32[2]{0:T(128)S(1)}, s32[2]{0:T(128)}, u32[]{:S(2)}) copy-start(s32[2]{0:T(128)} %param.10) | copy-start | bytes 28
  70.8 56.1 %all-gather.12.cloned.1.call-start = ((), (), s32[]{:S(2)}) async-start(), calls=%async_computation.9 | async-start | bytes 1474560 | tf_op jit(solution)/shard_map/all_gather | solution.py:45
  109.3 98.7 %all-gather.8.cloned.1.call-start = ((), (), s32[]{:S(2)}) async-start(), calls=%async_computation.7 | async-start | bytes 1474560 | tf_op jit(solution)/shard_map/all_gather | solution.py:45
  109.9 178.1 %reduce-scatter.25.cloned.1.call-start = ((), (), s32[]{:S(2)}) async-start(), calls=%async_computation.14 | async-start | bytes 1474560
  207.9 105.8 %reduce-scatter.21.cloned.1.call-start = ((), (), s32[]{:S(2)}) async-start(), calls=%async_computation.12 | async-start | bytes 1474560
  266.9 51.7 %copy-start.5 = (s32[16]{0:T(128)S(1)}, s32[16]{0:T(128)}, u32[]{:S(2)}) copy-start(s32[16]{0:T(128)} %param.11) | copy-start | bytes 196
  287.9 47.5 %all-gather.10.cloned.1.call-start = ((), (), s32[]{:S(2)}) async-start(), calls=%async_computation.8 | async-start | bytes 1474560 | tf_op jit(solution)/shard_map/all_gather | solution.py:45
  317.8 37.3 %all-gather.14.cloned.1.call-start = ((), (), s32[]{:S(2)}) async-start(), calls=%async_computation.10 | async-start | bytes 1474560 | tf_op jit(solution)/shard_map/all_gather | solution.py:45
  318.5 372.1 %reduce-scatter.29.cloned.1.call-start = ((), (), s32[]{:S(2)}) async-start(), calls=%async_computation.16 | async-start | bytes 18579456
  413.3 557.8 %reduce-scatter.27.cloned.1.call-start = ((), (), s32[]{:S(2)}) async-start(), calls=%async_computation.15 | async-start | bytes 18579456
  519.9 0.7 copy-start.6
Sparse Core Ops, SparseCore 0:
  9.6 24.2 all-gather.5
  50.4 25.7 reduce-scatter.18
  79.5 25.7 reduce-scatter.22
  109.4 17.4 all-gather.11
  128.3 17.4 all-gather.7
  208.1 25.7 reduce-scatter.24
  288.0 25.6 reduce-scatter.20
  317.9 17.4 all-gather.9
  337.6 17.4 all-gather.13
  413.5 277.0 reduce-scatter.28
  694.6 276.5 reduce-scatter.26
where the time goes:
time: 1000 us; the launch traced here: 992 us
  waiting for transfers between devices  546 us (55%)
  matrix products  323 us (32%)
  local copies, waits for them, and re-layouts  90.5 us (9%)
  other arithmetic  16 us (2%)
  between operations  15.1 us (2%)
    unnamed x17, waiting for transfers between devices  482 us
    dot_general x8, matrix products, contract_rows(): lax.dot_general(former, latter, (((0,), (0,)), ((), ())), preferred_eleme...  222 us
    unnamed x30, local copies, waits for them, and re-layouts  89.3 us
    dot_general x4, matrix products, contract_cols(): lax.dot_general(former, latter, (((1,), (1,)), ((), ())), preferred_eleme...  50.6 us
    dot_general x4, matrix products, local_pass(): jnp.dot(hidden, weight_down, preferred_element_type=jnp.float32)  50.3 us
    all_gather x4, waiting for transfers between devices, local_pass(): residual = lax.all_gather(residual, 'tensor', axis=1, tiled=True)  38.2 us
    all_gather x1, waiting for transfers between devices, on_device(): gathered = lax.all_gather(tokens, 'tensor', axis=2, tiled=True)  25.9 us
  transfers between devices with their start and end apart: 11, of which 9 were waited for; matrix products, arithmetic and copies ran while one was open for 33% of the time, Pallas kernels for 0%

commit v1 on v0

v1 whole, which is shorter than its diff:
```python
import jax
import jax.numpy as jnp
from jax import lax
from jax.sharding import PartitionSpec as P

STEPS = 2
PAIR = 2

client_rate = 0.0003
momentum_decay = 0.9


def silu_slope(preact):
    logistic = jax.nn.sigmoid(preact)
    return logistic * (1.0 + preact * (1.0 - logistic))


def contract_cols(former, latter):
    return lax.dot_general(
        former, latter, (((1,), (1,)), ((), ())), preferred_element_type=jnp.float32
    )


def by_client(array, clients):
    return array.reshape(clients, array.shape[0] // clients, array.shape[1])


def gram(former, latter, clients):
    return jnp.einsum(
        "crk,cqk->crq",
        by_client(former, clients),
        by_client(latter, clients),
        preferred_element_type=jnp.float32,
    )


def correction(grams, factor, clients):
    wide = jnp.einsum(
        "crq,cqk->crk",
        client_rate * grams,
        by_client(factor, clients).astype(jnp.float32),
        precision=lax.Precision.HIGHEST,
        preferred_element_type=jnp.float32,
    )
    return wide.reshape(factor.shape)


def on_device(
    group_size,
    tokens,
    targets,
    token_counts,
    sample_counts,
    up_weight,
    down_weight,
    momentum_up,
    momentum_down,
):
    clients, row_count, own_width = tokens.shape
    hidden_count, width = up_weight.shape
    rows = clients * row_count
    block = width // group_size
    lines = group_size // PAIR
    group = lax.axis_index("group")
    low = lax.rem(group, PAIR)
    across = [(g, g ^ 1) for g in range(group_size)]

    def to_partner(array):
        return lax.ppermute(array, "group", across)

    def gather_cols(array):
        return lax.all_gather(array, "tensor", axis=1, tiled=True)

    inputs = gather_cols(tokens.reshape(rows, own_width))
    own_target = targets.reshape(rows, own_width).astype(jnp.float32)
    positions = jnp.arange(row_count, dtype=jnp.int32)[None, :]
    row_mask = (positions < token_counts[:, None]).astype(jnp.float32).reshape(rows, 1)
    client_weights = lax.dynamic_slice_in_dim(sample_counts, group * clients, clients).astype(
        jnp.float32
    )
    row_weight = jnp.repeat(client_weights, row_count)[:, None]

    def residual_of(partial_out):
        own_cols = lax.psum_scatter(
            partial_out.astype(jnp.bfloat16), "tensor", scatter_dimension=1, tiled=True
        ).astype(jnp.float32)
        return gather_cols((row_mask * (own_cols - own_target)).astype(jnp.bfloat16))

    def column_sets(factor):
        weighted = (row_weight * factor.astype(jnp.float32)).astype(jnp.bfloat16)
        sets = weighted.reshape(rows, lines, PAIR, block).transpose(2, 1, 0, 3)
        mine = lax.dynamic_index_in_dim(sets, low, 0, keepdims=False)
        other = lax.dynamic_index_in_dim(sets, 1 - low, 0, keepdims=False)
        return mine, to_partner(other)

    preact0 = contract_cols(inputs, up_weight)
    hidden0 = jax.nn.silu(preact0).astype(jnp.bfloat16)
    partial0 = jnp.dot(hidden0, down_weight, preferred_element_type=jnp.float32)
    hidden0_far = to_partner(hidden0)
    input_grams = gram(inputs, inputs, clients)
    input_cols = column_sets(inputs)
    residual0 = residual_of(partial0)
    slopes0 = (contract_cols(residual0, down_weight) * silu_slope(preact0)).astype(jnp.bfloat16)
    slopes0_far = to_partner(slopes0)

    preact1 = preact0 - correction(input_grams, slopes0, clients)
    hidden1 = jax.nn.silu(preact1).astype(jnp.bfloat16)
    partial1 = jnp.dot(
        hidden1, down_weight, preferred_element_type=jnp.float32
    ) - correction(gram(hidden1, hidden0, clients), residual0, clients)
    hidden1_far = to_partner(hidden1)
    residual0_cols = column_sets(residual0)
    residual1 = residual_of(partial1)
    residual1_cols = column_sets(residual1)
    back1 = contract_cols(residual1, down_weight) - correction(
        gram(residual1, residual0, clients), hidden0, clients
    )
    slopes1 = (back1 * silu_slope(preact1)).astype(jnp.bfloat16)
    slopes1_far = to_partner(slopes1)

    weight_total = jnp.sum(sample_counts).astype(jnp.float32)
    alike = [[line * PAIR + part for line in range(lines)] for part in range(PAIR)]

    def server_sum(left, right):
        pair_sum = jnp.einsum(
            "kf,nkc->nfc",
            jnp.concatenate(left, axis=0),
            jnp.concatenate(right, axis=1),
            preferred_element_type=jnp.float32,
        ).astype(jnp.bfloat16)
        return lax.psum_scatter(
            pair_sum.reshape(lines * hidden_count, block),
            "group",
            scatter_dimension=0,
            axis_index_groups=alike,
            tiled=True,
        ).astype(jnp.float32)

    sum_down = server_sum(
        (hidden0, hidden1, hidden0_far, hidden1_far),
        (residual0_cols[0], residual1_cols[0], residual0_cols[1], residual1_cols[1]),
    )
    sum_up = server_sum(
        (slopes0, slopes1, slopes0_far, slopes1_far),
        (input_cols[0], input_cols[0], input_cols[1], input_cols[1]),
    )
    new_momentum_up = momentum_decay * momentum_up + sum_up / weight_total
    new_momentum_down = momentum_decay * momentum_down + sum_down / weight_total
    return (new_momentum_up, new_momentum_down)


def solution(mesh):
    placed = (
        P("group", None, "tensor"),
        P("group", None, "tensor"),
        P("group"),
        P(),
        P("tensor", None),
        P("tensor", None),
        P("tensor", "group"),
        P("tensor", "group"),
    )
    group_size = mesh.shape["group"]

    def run(*args):
        return on_device(group_size, *args)

    return jax.shard_map(
        run,
        mesh=mesh,
        in_specs=placed,
        out_specs=(P("tensor", "group"), P("tensor", "group")),
        check_vma=False,
    )
```

time: 1000 us -> 629 us (0.63)
  matrix products: 323 us -> 90.9 us
  waiting for transfers between devices: 546 us -> 425 us
  local copies, waits for them, and re-layouts: 90.5 us -> 58 us
    unnamed x17 -> x11, waiting for transfers between devices: 482 us -> 246 us
    dot_general x12 -> x10, matrix products: 273 us -> 56.9 us  [the longest x2 25.1 us: server_sum(): jnp.einsum('kf,nkc->nfc', jnp.concatenate(left, axis=0), jnp.concatenate(...]
    ppermute x0 -> x7, waiting for transfers between devices: none -> 111 us  [to_partner(): return lax.ppermute(array, 'group', across)]
    unnamed x30 -> x50, local copies, waits for them, and re-layouts: 89.3 us -> 43.5 us
    dot_general x4 -> x3, matrix products: 50.6 us -> 34 us  [contract_cols(): lax.dot_general(former, latter, (((1,), (1,)), ((), ())), preferred_eleme...]
    all_gather x5 -> x3, waiting for transfers between devices: 64.1 us -> 67.2 us  [gather_cols(): return lax.all_gather(array, 'tensor', axis=1, tiled=True)]
  transfers between devices with their start and end apart: 11 -> 14, of which waited for: 9 -> 10; matrix products, arithmetic and copies ran while one was open for 33% -> 10% of each run, Pallas kernels for 0% -> 0%
where the time goes in v1:
time: 629 us; the launch traced here: 620 us
  waiting for transfers between devices  425 us (68%)
  matrix products  90.9 us (14%)
  local copies, waits for them, and re-layouts  58 us (9%)
  other arithmetic  21.4 us (3%)
  between operations  15.5 us (2%)
  starting transfers between devices  9.55 us (2%)
    unnamed x11, waiting for transfers between devices  246 us
    ppermute x7, waiting for transfers between devices, to_partner(): return lax.ppermute(array, 'group', across)  111 us
    all_gather x3, waiting for transfers between devices, gather_cols(): return lax.all_gather(array, 'tensor', axis=1, tiled=True)  67.2 us
    unnamed x50, local copies, waits for them, and re-layouts  43.5 us
    dot_general x3, matrix products, contract_cols(): lax.dot_general(former, latter, (((1,), (1,)), ((), ())), preferred_eleme...  34 us
    dot_general x2, matrix products, server_sum(): jnp.einsum('kf,nkc->nfc', jnp.concatenate(left, axis=0), jnp.concatenate(...  25.1 us
  transfers between devices with their start and end apart: 14, of which 10 were waited for; matrix products, arithmetic and copies ran while one was open for 10% of the time, Pallas kernels for 0%

profile of v1, /device:TPU:10, one launch (start us, length us, event | category | flops | bytes accessed | tf_op | source)
XLA Modules:
  0.0 620.0 jit_solution(4506173377261697590)
XLA Ops:
  7.2 2.1 copy.56
  9.4 25.1 %all-gather.4.cloned.1.call-done = bf16[256,4608]{0,1:T(8,128)(2,1)} async-done(((bf16[256,1152]{0,1:T(8,128)(2,1)}), bf16[256,4608]{0,1:T(8,128)(2,1)}) %all-gather.4.cloned.1.call-update) | async-done | bytes 2359312 | tf_op jit(solution)/shard_map/all_gather | solution.py:72
  34.5 12.0 %multiply_convert_fusion.4 = (bf16[256,1728]{0,1:T(8,128)(2,1)S(1)}, f32[256,1728]{0,1:T(8,128)}) fusion(bf16[1728,4608]{1,0:T(8,128)(2,1)} %param.12, bf16[256,4608]{0,1:T(8,128)(2,1)} %all-gather.4.cloned.1.call-done), kind=kOutput, calls=%fused_computation.46 | convolution fusion | flops 4079075328 | bytes 20938752 | tf_op jit(solution)/shard_map/dot_general | solution.py:19
  47.4 10.3 %convolution_convert_fusion = bf16[256,4608]{1,0:T(8,128)(2,1)S(1)} fusion(bf16[256,1728]{0,1:T(8,128)(2,1)S(1)} %get-tuple-element.11, bf16[1728,4608]{1,0:T(8,128)(2,1)} %param.13), kind=kOutput, calls=%fused_computation.4 | convolution fusion | flops 4078043136 | bytes 19169280 | tf_op jit(solution)/shard_map/dot_general | solution.py:98
  57.7 2.4 copy.58
  61.8 31.6 %reduce-scatter.13.cloned.1.call-done = bf16[1152,256]{1,0:T(8,128)(2,1)} async-done(((bf16[4608,256]{1,0:T(8,128)(2,1)}), bf16[1152,256]{1,0:T(8,128)(2,1)}) %reduce-scatter.13.cloned.1.call-update) | async-done | bytes 589840
  95.7 2.8 copy.40
  99.9 19.8 %all-gather.6.cloned.1.call-done = bf16[256,4608]{0,1:T(8,128)(2,1)} async-done(((bf16[256,1152]{0,1:T(8,128)(2,1)}), bf16[256,4608]{0,1:T(8,128)(2,1)}) %all-gather.6.cloned.1.call-update) | async-done | bytes 2359312 | tf_op jit(solution)/shard_map/all_gather | solution.py:72
  119.7 11.5 %fusion.28 = bf16[256,1728]{0,1:T(8,128)(2,1)S(1)} fusion(bf16[1728,4608]{1,0:T(8,128)(2,1)} %param.13, bf16[256,4608]{0,1:T(8,128)(2,1)} %all-gather.6.cloned.1.call-done, f32[256,1728]{0,1:T(8,128)} %get-tuple-element.12), kind=kOutput, calls=%fused_computation.41 | convolution fusion | flops 4080844800 | bytes 20938752 | tf_op jit(solution)/shard_map/dot_general | solution.py:19
  136.3 2.8 copy.45
  139.1 3.1 fusion.41
  142.3 11.5 %fusion = bf16[256,4608]{1,0:T(8,128)(2,1)} fusion(f32[256,4608]{1,0:T(8,128)S(1)} %bitcast.132, bf16[256,1728]{0,1:T(8,128)(2,1)S(1)} %copy-done.9, bf16[1728,4608]{1,0:T(8,128)(2,1)} %param.13), kind=kOutput, calls=%fused_computation.3 | convolution fusion | flops 4079222784 | bytes 23887872 | tf_op jit(solution)/shard_map/dot_general | solution.py:108
  153.8 4.3 copy.60
  158.1 33.1 %reduce-scatter.15.cloned.1.call-done = bf16[1152,256]{1,0:T(8,128)(2,1)} async-done(((bf16[4608,256]{1,0:T(8,128)(2,1)}), bf16[1152,256]{1,0:T(8,128)(2,1)}) %reduce-scatter.15.cloned.1.call-update) | async-done | bytes 589840
  195.2 22.3 %all-gather.8.cloned.1.call-done = bf16[256,4608]{0,1:T(8,128)(2,1)} async-done(((bf16[256,1152]{0,1:T(8,128)(2,1)}), bf16[256,4608]{0,1:T(8,128)(2,1)}) %all-gather.8.cloned.1.call-update) | async-done | bytes 2359312 | tf_op jit(solution)/shard_map/all_gather | solution.py:72
  217.5 6.6 %multiply_convert_fusion.1 = (bf16[256,4608]{0,1:T(8,128)(2,1)}, bf16[256,4608]{0,1:T(8,128)(2,1)}, bf16[256,4608]{0,1:T(8,128)(2,1)S(1)}) fusion(bf16[256,4608]{0,1:T(8,128)(2,1)} %all-gather.6.cloned.1.call-done, f32[256]{0:T(256)S(1)} %broadcast_bitcast_fusion, bf16[256,4608]{0,1:T(8,128)(2,1)} %all-gather.8.cloned.1.call-done, ...), kind=kLoop, calls=%fused_computation.20 | loop fusion | flops 10616832 | bytes 14156800 | tf_op jit(solution)/shard_map/convert_element_type | solution.py:90
  227.2 4.3 copy.47
  231.5 2.6 convolution_multiply_fusion.1
  235.8 10.5 %fusion.29 = bf16[256,1728]{0,1:T(8,128)(2,1)S(1)} fusion(bf16[1728,4608]{1,0:T(8,128)(2,1)} %param.13, bf16[256,4608]{0,1:T(8,128)(2,1)S(1)} %copy-done, f32[2,216,8,128]{3,2,1,0:T(8,128)S(1)} %convolution_bitcast_fusion, f32[256,1728]{0,1:T(8,128)S(1)} %copy-done.12, f32[2,216,8,128]{3,2,1,0:T(8,128)S(1)} %copy-done.4), kind=kOutput, calls=%fused_computation.42 | convolution fusion | flops 4081729536 | bytes 24477696 | tf_op jit(solution)/shard_map/dot_general | solution.py:19
  247.0 26.0 %collective-permute-done.2 = bf16[256,1728]{0,1:T(8,128)(2,1)S(1)} collective-permute-done((bf16[256,1728]{0,1:T(8,128)(2,1)S(1)}, bf16[256,1728]{0,1:T(8,128)(2,1)S(1)}, u32[]{:S(2)}, u32[]{:S(2)}) %collective-permute-start.2) | collective-permute-done | bytes 884768 | tf_op jit(solution)/shard_map/ppermute | solution.py:69
  273.0 12.6 %convert_bitcast_fusion.1 = bf16[4,1728,576]{1,2,0:T(8,128)(2,1)} fusion(bf16[4,256,576]{1,2,0:T(8,128)(2,1)} %collective-permute-done, bf16[4,256,576]{1,2,0:T(8,128)(2,1)S(1)} %copy-done.13, bf16[256,1728]{0,1:T(8,128)(2,1)S(1)} %collective-permute-done.2, bf16[256,1728]{0,1:T(8,128)(2,1)} %collective-permute-done.1, bf16[256,1728]{0,1:T(8,128)(2,1)S(1)} %fusion.29, ...), kind=kOutput, calls=%fused_computation.1 | convolution fusion | flops 8190738432 | bytes 13860864 | tf_op jit(solution)/shard_map/kf,nkc->nfc/dot_general | solution.py:125
  285.6 11.7 %copy.66 = bf16[4,1728,576]{2,1,0:T(8,128)(2,1)} copy(bf16[4,1728,576]{1,2,0:T(8,128)(2,1)} %convert_bitcast_fusion.1) | data formatting | bytes 15925248
  304.3 68.0 %collective-permute-done.5 = bf16[256,1728]{0,1:T(8,128)(2,1)S(1)} collective-permute-done((bf16[256,1728]{0,1:T(8,128)(2,1)S(1)}, bf16[256,1728]{0,1:T(8,128)(2,1)S(1)}, u32[]{:S(2)}, u32[]{:S(2)}) %collective-permute-start.5) | collective-permute-done | bytes 884768 | tf_op jit(solution)/shard_map/ppermute | solution.py:69
  372.3 17.3 %collective-permute-done.6 = bf16[256,1728]{0,1:T(8,128)(2,1)S(1)} collective-permute-done((bf16[256,1728]{0,1:T(8,128)(2,1)S(1)}, bf16[256,1728]{0,1:T(8,128)(2,1)S(1)}, u32[]{:S(2)}, u32[]{:S(2)}) %collective-permute-start.6) | collective-permute-done | bytes 884768 | tf_op jit(solution)/shard_map/ppermute | solution.py:69
  390.6 12.6 %convert_bitcast_fusion = bf16[4,1728,576]{1,2,0:T(8,128)(2,1)} fusion(bf16[4,256,576]{1,2,0:T(8,128)(2,1)S(1)} %collective-permute-done.4, bf16[4,256,576]{1,2,0:T(8,128)(2,1)S(1)} %collective-permute-done.3, bf16[4,256,576]{1,2,0:T(8,128)(2,1)S(1)} %get-tuple-element.4, bf16[4,256,576]{1,2,0:T(8,128)(2,1)S(1)} %get-tuple-element.2, ...), kind=kOutput, calls=%fused_computation | convolution fusion | flops 8190738432 | bytes 16220160 | tf_op jit(solution)/shard_map/kf,nkc->nfc/dot_general | solution.py:125
  403.1 11.7 %copy.67 = bf16[4,1728,576]{2,1,0:T(8,128)(2,1)} copy(bf16[4,1728,576]{1,2,0:T(8,128)(2,1)} %convert_bitcast_fusion) | data formatting | bytes 15925248
  416.1 33.8 %reduce-scatter.17.cloned.1.call-done = bf16[1728,576]{1,0:T(8,128)(2,1)} async-done(((bf16[6912,576]{1,0:T(8,128)(2,1)}), bf16[1728,576]{1,0:T(8,128)(2,1)}) %reduce-scatter.17.cloned.1.call-update) | async-done | bytes 1990672
  449.9 2.9 copy.63
  452.9 4.7 divide_add_fusion.1
  457.6 147.4 %reduce-scatter.19.cloned.1.call-done = bf16[1728,576]{1,0:T(8,128)(2,1)} async-done(((bf16[6912,576]{1,0:T(8,128)(2,1)}), bf16[1728,576]{1,0:T(8,128)(2,1)}) %reduce-scatter.19.cloned.1.call-update) | async-done | bytes 1990672
  605.0 2.9 copy.65
  608.0 4.7 divide_add_fusion
  (85 shorter events, 29.3 us)
Async XLA Ops:
  7.2 27.3 %all-gather.4.cloned.1.call-start = ((), (), s32[]{:S(2)}) async-start(), calls=%async_computation.4 | async-start | bytes 2949120 | tf_op jit(solution)/shard_map/all_gather | solution.py:72
  9.4 84.0 %reduce-scatter.13.cloned.1.call-start = ((), (), s32[]{:S(2)}) async-start(), calls=%async_computation.7 | async-start | bytes 2949120
  60.2 1.5 copy-start.20
  60.2 59.5 %all-gather.6.cloned.1.call-start = ((), (), s32[]{:S(2)}) async-start(), calls=%async_computation.5 | async-start | bytes 2949120 | tf_op jit(solution)/shard_map/all_gather | solution.py:72
  95.4 95.8 %reduce-scatter.15.cloned.1.call-start = ((), (), s32[]{:S(2)}) async-start(), calls=%async_computation.8 | async-start | bytes 2949120
  119.7 11.5 %copy-start.17 = (f32[2,128,128]{2,1,0:T(8,128)S(1)}, f32[2,128,128]{2,1,0:T(8,128)}, u32[]{:S(2)}) copy-start(f32[2,128,128]{2,1,0:T(8,128)} %convolution_multiply_fusion.2) | copy-start | bytes 393220
  131.2 2.3 copy-start.14
  131.2 1.8 copy-start.11
  133.0 1.2 copy-start.3
  133.0 2.1 copy-start.6
  139.1 3.1 copy-start.9
  158.0 35.6 %copy-start.21 = (s32[16]{0:T(128)S(1)}, s32[16]{0:T(128)}, u32[]{:S(2)}) copy-start(s32[16]{0:T(128)} %param.11) | copy-start | bytes 196
  158.0 59.5 %all-gather.8.cloned.1.call-start = ((), (), s32[]{:S(2)}) async-start(), calls=%async_computation.6 | async-start | bytes 2949120 | tf_op jit(solution)/shard_map/all_gather | solution.py:72
  193.3 256.6 %reduce-scatter.17.cloned.1.call-start = ((), (), s32[]{:S(2)}) async-start(), calls=%async_computation.9 | async-start | bytes 11059200
  193.7 53.2 %collective-permute-start.1 = (bf16[256,1728]{0,1:T(8,128)(2,1)}, bf16[256,1728]{0,1:T(8,128)(2,1)}, u32[]{:S(2)}, u32[]{:S(2)}) collective-permute-start(bf16[256,1728]{0,1:T(8,128)(2,1)} %copy-done.14), channel_id=1, source_target_pairs={{0,4},{4,0},{8,12},{12,8},{16,20},{20,16},{24,28},{28,24},{1,5},{5... | collective-permute-start | bytes 2654216 | tf_op jit(solution)/shard_map/ppermute | solution.py:69
  225.7 47.3 %collective-permute-start = (bf16[4,256,576]{1,2,0:T(8,128)(2,1)}, bf16[4,256,576]{1,2,0:T(8,128)(2,1)}, u32[]{:S(2)}, u32[]{:S(2)}) collective-permute-start(bf16[4,256,576]{1,2,0:T(8,128)(2,1)} %get-tuple-element.7), channel_id=1, source_target_pairs={{0,4},{4,0},{8,12},{12,8},{16,20},{20,16},{24,28},{28,24},{1,5},{5... | collective-permute-start | bytes 3538952 | tf_op jit(solution)/shard_map/ppermute | solution.py:69
  231.5 2.6 copy-start.7
  231.5 3.5 copy-start.4
  231.5 3.5 copy-start.12
  234.1 1.8 copy-start
  235.8 37.1 %copy-start.13 = (bf16[4,256,576]{1,2,0:T(8,128)(2,1)S(1)}, bf16[4,256,576]{1,2,0:T(8,128)(2,1)}, u32[]{:S(2)}) copy-start(bf16[4,256,576]{1,2,0:T(8,128)(2,1)} %get-tuple-element.6) | copy-start | bytes 3538948
  235.8 37.1 %copy-start.15 = (bf16[256,1728]{0,1:T(8,128)(2,1)S(1)}, bf16[256,1728]{0,1:T(8,128)(2,1)}, u32[]{:S(2)}) copy-start(bf16[256,1728]{0,1:T(8,128)(2,1)} %copy-done.14) | copy-start | bytes 2654212
  246.3 26.6 %collective-permute-start.2 = (bf16[256,1728]{0,1:T(8,128)(2,1)S(1)}, bf16[256,1728]{0,1:T(8,128)(2,1)S(1)}, u32[]{:S(2)}, u32[]{:S(2)}) collective-permute-start(bf16[256,1728]{0,1:T(8,128)(2,1)S(1)} %fusion.29), channel_id=1, source_target_pairs={{0,4},{4,0},{8,12},{12,8},{16,20},{20,16},{24,28},{28,24},{1,5},{5... | collective-permute-start | bytes 2654216 | tf_op jit(solution)/shard_map/ppermute | solution.py:69
  297.3 1.7 copy-start.2
  297.3 307.7 %reduce-scatter.19.cloned.1.call-start = ((), (), s32[]{:S(2)}) async-start(), calls=%async_computation.10 | async-start | bytes 11059200
  298.9 1.7 copy-start.1
  299.1 90.6 %collective-permute-start.4 = (bf16[4,256,576]{1,2,0:T(8,128)(2,1)S(1)}, bf16[4,256,576]{1,2,0:T(8,128)(2,1)S(1)}, u32[]{:S(2)}, u32[]{:S(2)}) collective-permute-start(bf16[4,256,576]{1,2,0:T(8,128)(2,1)S(1)} %get-tuple-element.5), channel_id=1, source_target_pairs={{0,4},{4,0},{8,12},{12,8},{16,20},{20,16},{24,28},{28,24},{1,5},{5... | collective-permute-start | bytes 3538952 | tf_op jit(solution)/shard_map/ppermute | solution.py:69
  300.6 2.3 copy-start.10
  300.8 88.9 %collective-permute-start.3 = (bf16[4,256,576]{1,2,0:T(8,128)(2,1)S(1)}, bf16[4,256,576]{1,2,0:T(8,128)(2,1)S(1)}, u32[]{:S(2)}, u32[]{:S(2)}) collective-permute-start(bf16[4,256,576]{1,2,0:T(8,128)(2,1)S(1)} %get-tuple-element.3), channel_id=1, source_target_pairs={{0,4},{4,0},{8,12},{12,8},{16,20},{20,16},{24,28},{28,24},{1,5},{5... | collective-permute-start | bytes 3538952 | tf_op jit(solution)/shard_map/ppermute | solution.py:69
  302.3 70.0 %collective-permute-start.5 = (bf16[256,1728]{0,1:T(8,128)(2,1)S(1)}, bf16[256,1728]{0,1:T(8,128)(2,1)S(1)}, u32[]{:S(2)}, u32[]{:S(2)}) collective-permute-start(bf16[256,1728]{0,1:T(8,128)(2,1)S(1)} %copy-done.7), channel_id=1, source_target_pairs={{0,4},{4,0},{8,12},{12,8},{16,20},{20,16},{24,28},{28,24},{1,5},{5... | collective-permute-start | bytes 2654216 | tf_op jit(solution)/shard_map/ppermute | solution.py:69
  302.9 86.8 %collective-permute-start.6 = (bf16[256,1728]{0,1:T(8,128)(2,1)S(1)}, bf16[256,1728]{0,1:T(8,128)(2,1)S(1)}, u32[]{:S(2)}, u32[]{:S(2)}) collective-permute-start(bf16[256,1728]{0,1:T(8,128)(2,1)S(1)} %copy-done.10), channel_id=1, source_target_pairs={{0,4},{4,0},{8,12},{12,8},{16,20},{20,16},{24,28},{28,24},{1,5},{5... | collective-permute-start | bytes 2654216 | tf_op jit(solution)/shard_map/ppermute | solution.py:69
  372.3 17.4 %copy-start.18 = (bf16[256,1728]{0,1:T(8,128)(2,1)}, bf16[256,1728]{0,1:T(8,128)(2,1)S(1)}, u32[]{:S(2)}) copy-start(bf16[256,1728]{0,1:T(8,128)(2,1)S(1)} %collective-permute-done.5) | copy-start | bytes 2654212
  (4 other events, 3.8 us)
Sparse Core Ops, SparseCore 0:
  10.1 24.2 all-gather.3
  60.3 33.0 reduce-scatter.12
  95.6 24.0 all-gather.5
  158.2 33.0 reduce-scatter.14
  193.4 24.0 all-gather.7
  297.4 152.4 reduce-scatter.16
  452.4 152.5 reduce-scatter.18

commit v2 on v1

--- a/solution.py
+++ b/solution.py
@@ -80,11 +80,15 @@
     )
     row_weight = jnp.repeat(client_weights, row_count)[:, None]
 
-    def residual_of(partial_out):
+    def residual_of(partial_out, early, late):
         own_cols = lax.psum_scatter(
             partial_out.astype(jnp.bfloat16), "tensor", scatter_dimension=1, tiled=True
-        ).astype(jnp.float32)
-        return gather_cols((row_mask * (own_cols - own_target)).astype(jnp.bfloat16))
+        )
+        own_cols, early = lax.optimization_barrier((own_cols, early))
+        own_cols = own_cols.astype(jnp.float32)
+        whole = gather_cols((row_mask * (own_cols - own_target)).astype(jnp.bfloat16))
+        whole, late = lax.optimization_barrier((whole, late))
+        return whole, early, late
 
     def column_sets(factor):
         weighted = (row_weight * factor.astype(jnp.float32)).astype(jnp.bfloat16)
@@ -99,7 +103,7 @@
     hidden0_far = to_partner(hidden0)
     input_grams = gram(inputs, inputs, clients)
     input_cols = column_sets(inputs)
-    residual0 = residual_of(partial0)
+    residual0, hidden0_far, input_cols = residual_of(partial0, hidden0_far, input_cols)
     slopes0 = (contract_cols(residual0, down_weight) * silu_slope(preact0)).astype(jnp.bfloat16)
     slopes0_far = to_partner(slopes0)
 
@@ -110,7 +114,9 @@
     ) - correction(gram(hidden1, hidden0, clients), residual0, clients)
     hidden1_far = to_partner(hidden1)
     residual0_cols = column_sets(residual0)
-    residual1 = residual_of(partial1)
+    residual1, (hidden1_far, slopes0_far), residual0_cols = residual_of(
+        partial1, (hidden1_far, slopes0_far), residual0_cols
+    )
     residual1_cols = column_sets(residual1)
     back1 = contract_cols(residual1, down_weight) - correction(
         gram(residual1, residual0, clients), hidden0, clients
@@ -123,18 +129,18 @@
 
     def server_sum(left, right):
         pair_sum = jnp.einsum(
-            "kf,nkc->nfc",
+            "nkc,kf->ncf",
+            jnp.concatenate(right, axis=1),
             jnp.concatenate(left, axis=0),
-            jnp.concatenate(right, axis=1),
             preferred_element_type=jnp.float32,
         ).astype(jnp.bfloat16)
         return lax.psum_scatter(
-            pair_sum.reshape(lines * hidden_count, block),
+            pair_sum.reshape(lines * block, hidden_count),
             "group",
             scatter_dimension=0,
             axis_index_groups=alike,
             tiled=True,
-        ).astype(jnp.float32)
+        ).T.astype(jnp.float32)
 
     sum_down = server_sum(
         (hidden0, hidden1, hidden0_far, hidden1_far),

time: 629 us -> 600 us (0.954)
  local copies, waits for them, and re-layouts: 58 us -> 31.8 us
    reduce_scatter x0 -> x2, waiting for transfers between devices: none -> 244 us  [server_sum(): lax.psum_scatter(pair_sum.reshape(lines * block, hidden_count), 'group',...]
    unnamed x11 -> x9, waiting for transfers between devices: 246 us -> 62 us
    all_gather x3, waiting for transfers between devices: 67.2 us -> 25.1 us  [gather_cols(): return lax.all_gather(array, 'tensor', axis=1, tiled=True)]
    unnamed x50 -> x42, local copies, waits for them, and re-layouts: 43.5 us -> 7.68 us
    ppermute x7, waiting for transfers between devices: 111 us -> 91.4 us  [to_partner(): return lax.ppermute(array, 'group', across)]
    optimization_barrier x0 -> x4, local copies, waits for them, and re-layouts: none -> 8.62 us  [residual_of(): own_cols, early = lax.optimization_barrier((own_cols, early))]
    all_gather x3 -> x1, local copies, waits for them, and re-layouts: 9.97 us -> 2.83 us  [gather_cols(): return lax.all_gather(array, 'tensor', axis=1, tiled=True)]
    reshape x0 -> x2, local copies, waits for them, and re-layouts: none -> 7.1 us  [by_client(): return array.reshape(clients, array.shape[0] // clients, array.shape[1])]
  transfers between devices with their start and end apart: 14 -> 14, of which waited for: 10 -> 10; matrix products, arithmetic and copies ran while one was open for 10% -> 6% of each run, Pallas kernels for 0% -> 0%
where the time goes in v2:
time: 600 us; the launch traced here: 591 us
  waiting for transfers between devices  423 us (70%)
  matrix products  91 us (15%)
  local copies, waits for them, and re-layouts  31.8 us (5%)
  other arithmetic  19.2 us (3%)
  between operations  15.5 us (3%)
  starting transfers between devices  10.5 us (2%)
    reduce_scatter x2, waiting for transfers between devices, server_sum(): lax.psum_scatter(pair_sum.reshape(lines * block, hidden_count), 'group',...  244 us
    ppermute x7, waiting for transfers between devices, to_partner(): return lax.ppermute(array, 'group', across)  91.4 us
    unnamed x9, waiting for transfers between devices  62 us
    dot_general x3, matrix products, contract_cols(): lax.dot_general(former, latter, (((1,), (1,)), ((), ())), preferred_eleme...  34.4 us
    dot_general x2, matrix products, server_sum(): jnp.einsum('nkc,kf->ncf', jnp.concatenate(right, axis=1), jnp.concatenate...  25.5 us
    all_gather x3, waiting for transfers between devices, gather_cols(): return lax.all_gather(array, 'tensor', axis=1, tiled=True)  25.1 us
  transfers between devices with their start and end apart: 14, of which 10 were waited for; matrix products, arithmetic and copies ran while one was open for 6% of the time, Pallas kernels for 0%

profile of v2, /device:TPU:10, one launch (start us, length us, event | category | flops | bytes accessed | tf_op | source)
XLA Modules:
  0.0 590.6 jit_solution(4025643088332300568)
XLA Ops:
  7.2 2.1 copy.53
  9.4 25.1 %all-gather.4.cloned.1.call-done = bf16[256,4608]{0,1:T(8,128)(2,1)} async-done(((bf16[256,1152]{0,1:T(8,128)(2,1)}), bf16[256,4608]{0,1:T(8,128)(2,1)}) %all-gather.4.cloned.1.call-update) | async-done | bytes 2359312 | tf_op jit(solution)/shard_map/all_gather | solution.py:72
  34.5 12.4 %multiply_convert_fusion.4 = (bf16[256,1728]{0,1:T(8,128)(2,1)}, f32[256,1728]{0,1:T(8,128)}) fusion(bf16[1728,4608]{1,0:T(8,128)(2,1)} %param.12, bf16[256,4608]{0,1:T(8,128)(2,1)} %all-gather.4.cloned.1.call-done), kind=kOutput, calls=%fused_computation.46 | convolution fusion | flops 4079075328 | bytes 20938752 | tf_op jit(solution)/shard_map/dot_general | solution.py:19
  46.8 10.3 %convolution_convert_fusion = bf16[256,4608]{1,0:T(8,128)(2,1)S(1)} fusion(bf16[256,1728]{0,1:T(8,128)(2,1)} %get-tuple-element.30, bf16[1728,4608]{1,0:T(8,128)(2,1)} %param.13), kind=kOutput, calls=%fused_computation.2 | convolution fusion | flops 4078043136 | bytes 19169280 | tf_op jit(solution)/shard_map/dot_general | solution.py:102
  57.1 2.4 copy.56
  61.8 31.0 %reduce-scatter.13.cloned.1.call-done = bf16[1152,256]{1,0:T(8,128)(2,1)} async-done(((bf16[4608,256]{1,0:T(8,128)(2,1)}), bf16[1152,256]{1,0:T(8,128)(2,1)}) %reduce-scatter.13.cloned.1.call-update) | async-done | bytes 589840
  94.9 2.3 copy.34
  103.2 2.8 copy.38
  107.5 22.3 %collective-permute-done.1 = bf16[4,256,576]{1,2,0:T(8,128)(2,1)} collective-permute-done((bf16[4,256,576]{1,2,0:T(8,128)(2,1)}, bf16[4,256,576]{1,2,0:T(8,128)(2,1)}, u32[]{:S(2)}, u32[]{:S(2)}) %collective-permute-start.1) | collective-permute-done | bytes 1179680 | tf_op jit(solution)/shard_map/ppermute | solution.py:69
  129.8 2.8 copy.60
  132.7 11.6 %fusion.28 = bf16[256,1728]{0,1:T(8,128)(2,1)S(1)} fusion(bf16[1728,4608]{1,0:T(8,128)(2,1)} %param.13, bf16[256,4608]{0,1:T(8,128)(2,1)} %all-gather.6.cloned.1.call-done, f32[256,1728]{0,1:T(8,128)} %get-tuple-element.31), kind=kOutput, calls=%fused_computation.41 | convolution fusion | flops 4080844800 | bytes 20938752 | tf_op jit(solution)/shard_map/dot_general | solution.py:19
  146.6 2.2 convolution_multiply_fusion.3
  148.8 4.1 fusion.41
  152.9 7.4 %fusion = bf16[256,4608]{1,0:T(8,128)(2,1)} fusion(f32[256,4608]{1,0:T(8,128)} %bitcast.128, bf16[256,1728]{0,1:T(8,128)(2,1)S(1)} %multiply_convert_fusion.3, bf16[1728,4608]{1,0:T(8,128)(2,1)S(1)} %bitcast.124), kind=kOutput, calls=%fused_computation.1 | convolution fusion | flops 4079222784 | bytes 23887872 | tf_op jit(solution)/shard_map/dot_general | solution.py:112
  160.4 4.3 copy.58
  167.0 30.9 %reduce-scatter.15.cloned.1.call-done = bf16[1152,256]{1,0:T(8,128)(2,1)} async-done(((bf16[4608,256]{1,0:T(8,128)(2,1)}), bf16[1152,256]{1,0:T(8,128)(2,1)}) %reduce-scatter.15.cloned.1.call-update) | async-done | bytes 589840
  200.0 4.8 collective-permute-done.3
  204.8 2.1 copy.44
  209.0 2.1 multiply_convert_fusion.1
  213.8 24.5 %collective-permute-done.4 = bf16[4,256,576]{1,2,0:T(8,128)(2,1)} collective-permute-done((bf16[4,256,576]{1,2,0:T(8,128)(2,1)S(1)}, bf16[4,256,576]{1,2,0:T(8,128)(2,1)}, u32[]{:S(2)}, u32[]{:S(2)}) %collective-permute-start.4) | collective-permute-done | bytes 1179680 | tf_op jit(solution)/shard_map/ppermute | solution.py:69
  238.3 4.3 copy.55
  242.6 2.6 convolution_multiply_fusion.1
  245.2 2.2 convolution_bitcast_fusion
  247.4 10.5 %fusion.29 = bf16[256,1728]{0,1:T(8,128)(2,1)S(1)} fusion(bf16[1728,4608]{1,0:T(8,128)(2,1)} %param.13, bf16[256,4608]{0,1:T(8,128)(2,1)S(1)} %copy-done.1, f32[2,216,8,128]{3,2,1,0:T(8,128)S(1)} %convolution_bitcast_fusion, f32[256,1728]{0,1:T(8,128)S(1)} %copy-done.7, f32[2,216,8,128]{3,2,1,0:T(8,128)S(1)} %copy-done.3), kind=kOutput, calls=%fused_computation.42 | convolution fusion | flops 4081729536 | bytes 24477696 | tf_op jit(solution)/shard_map/dot_general | solution.py:19
  259.4 17.2 %collective-permute-done.5 = bf16[256,1728]{0,1:T(8,128)(2,1)S(1)} collective-permute-done((bf16[256,1728]{0,1:T(8,128)(2,1)S(1)}, bf16[256,1728]{0,1:T(8,128)(2,1)S(1)}, u32[]{:S(2)}, u32[]{:S(2)}) %collective-permute-start.5) | collective-permute-done | bytes 884768 | tf_op jit(solution)/shard_map/ppermute | solution.py:69
  276.7 12.6 %convolution_convert_fusion.2 = bf16[4,576,1728]{2,1,0:T(8,128)(2,1)} fusion(bf16[4,256,576]{1,2,0:T(8,128)(2,1)} %collective-permute-done.1, bf16[4,256,576]{1,2,0:T(8,128)(2,1)S(1)} %copy-done.8, bf16[256,1728]{0,1:T(8,128)(2,1)S(1)} %collective-permute-done.5, bf16[256,1728]{0,1:T(8,128)(2,1)} %collective-permute-done.3, ...), kind=kOutput, calls=%fused_computation.4 | convolution fusion | flops 8190738432 | bytes 13860864 | tf_op jit(solution)/shard_map/nkc,kf->ncf/dot_general | solution.py:131
  291.8 22.6 %collective-permute-done.6 = bf16[4,256,576]{1,2,0:T(8,128)(2,1)S(1)} collective-permute-done((bf16[4,256,576]{1,2,0:T(8,128)(2,1)S(1)}, bf16[4,256,576]{1,2,0:T(8,128)(2,1)S(1)}, u32[]{:S(2)}, u32[]{:S(2)}) %collective-permute-start.6) | collective-permute-done | bytes 1179680 | tf_op jit(solution)/shard_map/ppermute | solution.py:69
  314.4 12.9 %convolution_convert_fusion.1 = bf16[4,576,1728]{2,1,0:T(8,128)(2,1)} fusion(bf16[4,256,576]{1,2,0:T(8,128)(2,1)S(1)} %collective-permute-done.6, bf16[4,256,576]{1,2,0:T(8,128)(2,1)} %collective-permute-done.4, bf16[4,256,576]{1,2,0:T(8,128)(2,1)S(1)} %get-tuple-element.24, bf16[4,256,576]{1,2,0:T(8,128)(2,1)S(1)} %copy-done.9, ...), kind=kOutput, calls=%fused_computation.3 | convolution fusion | flops 8190738432 | bytes 16220160 | tf_op jit(solution)/shard_map/nkc,kf->ncf/dot_general | solution.py:131
  328.6 103.7 %reduce-scatter.9.cloned.1.call-done = bf16[576,1728]{1,0:T(8,128)(2,1)} async-done(((bf16[2304,1728]{1,0:T(8,128)(2,1)}), bf16[576,1728]{1,0:T(8,128)(2,1)}) %reduce-scatter.9.cloned.1.call-update) | async-done | bytes 1990672 | tf_op jit(solution)/shard_map/reduce_scatter | solution.py:137
  432.4 5.3 bitcast_add_fusion.1
  437.7 140.3 %reduce-scatter.11.cloned.1.call-done = bf16[576,1728]{1,0:T(8,128)(2,1)} async-done(((bf16[2304,1728]{1,0:T(8,128)(2,1)}), bf16[576,1728]{1,0:T(8,128)(2,1)}) %reduce-scatter.11.cloned.1.call-update) | async-done | bytes 1990672 | tf_op jit(solution)/shard_map/reduce_scatter | solution.py:137
  578.0 5.3 bitcast_add_fusion
  (84 shorter events, 28.0 us)
Async XLA Ops:
  7.2 27.3 %all-gather.4.cloned.1.call-start = ((), (), s32[]{:S(2)}) async-start(), calls=%async_computation.4 | async-start | bytes 2949120 | tf_op jit(solution)/shard_map/all_gather | solution.py:72
  9.4 83.4 %reduce-scatter.13.cloned.1.call-start = ((), (), s32[]{:S(2)}) async-start(), calls=%async_computation.9 | async-start | bytes 2949120
  59.6 2.1 copy-start.14
  59.6 70.2 %all-gather.6.cloned.1.call-start = ((), (), s32[]{:S(2)}) async-start(), calls=%async_computation.5 | async-start | bytes 2949120 | tf_op jit(solution)/shard_map/all_gather | solution.py:72
  59.6 35.3 %collective-permute-start = (bf16[256,1728]{0,1:T(8,128)(2,1)}, bf16[256,1728]{0,1:T(8,128)(2,1)}, u32[]{:S(2)}, u32[]{:S(2)}) collective-permute-start(bf16[256,1728]{0,1:T(8,128)(2,1)} %get-tuple-element.30), channel_id=1, source_target_pairs={{0,4},{4,0},{8,12},{12,8},{16,20},{20,16},{24,28},{28,24},{1,5},{5... | collective-permute-start | bytes 2654216 | tf_op jit(solution)/shard_map/ppermute | solution.py:69
  94.9 4.6 copy-start.15
  94.9 4.7 copy-start
  99.2 98.7 %reduce-scatter.15.cloned.1.call-start = ((), (), s32[]{:S(2)}) async-start(), calls=%async_computation.10 | async-start | bytes 2949120
  101.8 28.0 %collective-permute-start.1 = (bf16[4,256,576]{1,2,0:T(8,128)(2,1)}, bf16[4,256,576]{1,2,0:T(8,128)(2,1)}, u32[]{:S(2)}, u32[]{:S(2)}) collective-permute-start(bf16[4,256,576]{1,2,0:T(8,128)(2,1)} %get-tuple-element.28), channel_id=1, source_target_pairs={{0,4},{4,0},{8,12},{12,8},{16,20},{20,16},{24,28},{28,24},{1,5},{5... | collective-permute-start | bytes 3538952 | tf_op jit(solution)/shard_map/ppermute | solution.py:69
  132.6 12.5 %copy-start.13 = (f32[2,128,128]{2,1,0:T(8,128)S(1)}, f32[2,128,128]{2,1,0:T(8,128)}, u32[]{:S(2)}) copy-start(f32[2,128,128]{2,1,0:T(8,128)} %convolution_multiply_fusion.2) | copy-start | bytes 393220
  132.6 13.4 %copy-start.6 = (f32[256,1728]{0,1:T(8,128)S(1)}, f32[256,1728]{0,1:T(8,128)}, u32[]{:S(2)}) copy-start(f32[256,1728]{0,1:T(8,128)} %get-tuple-element.31) | copy-start | bytes 5308420
  132.6 20.3 %slice-start = ((s8[15925248]{0:T(1024)(128)(4,1)}), s8[4194304]{0:T(1024)(128)(4,1)S(1)}, s32[]{:S(2)}) async-start(s8[15925248]{0:T(1024)(128)(4,1)} %bitcast.123), calls=%async_computation.11 | async-start | bytes 8388608
  132.6 20.3 %slice-start.1 = ((s8[15925248]{0:T(1024)(128)(4,1)}), s8[4194304]{0:T(1024)(128)(4,1)S(1)}, s32[]{:S(2)}) async-start(s8[15925248]{0:T(1024)(128)(4,1)} %bitcast.123), calls=%async_computation.12 | async-start | bytes 8388608
  132.7 20.3 %slice-start.2 = ((s8[15925248]{0:T(1024)(128)(4,1)}), s8[4194304]{0:T(1024)(128)(4,1)S(1)}, s32[]{:S(2)}) async-start(s8[15925248]{0:T(1024)(128)(4,1)} %bitcast.123), calls=%async_computation.13 | async-start | bytes 8388608
  145.2 7.8 %slice-start.3 = ((s8[15925248]{0:T(1024)(128)(4,1)}), s8[3342336]{0:T(1024)(128)(4,1)S(1)}, s32[]{:S(2)}) async-start(s8[15925248]{0:T(1024)(128)(4,1)} %bitcast.123), calls=%async_computation.14 | async-start | bytes 6684672
  146.0 2.7 copy-start.2
  146.6 6.3 %copy-start.4 = (bf16[256,1728]{0,1:T(8,128)(2,1)}, bf16[256,1728]{0,1:T(8,128)(2,1)S(1)}, u32[]{:S(2)}) copy-start(bf16[256,1728]{0,1:T(8,128)(2,1)S(1)} %multiply_convert_fusion.3) | copy-start | bytes 2654212
  164.7 73.7 %all-gather.8.cloned.1.call-start = ((), (), s32[]{:S(2)}) async-start(), calls=%async_computation.6 | async-start | bytes 2949120 | tf_op jit(solution)/shard_map/all_gather | solution.py:72
  164.9 35.1 %collective-permute-start.2 = (bf16[256,1728]{0,1:T(8,128)(2,1)}, bf16[256,1728]{0,1:T(8,128)(2,1)}, u32[]{:S(2)}, u32[]{:S(2)}) collective-permute-start(bf16[256,1728]{0,1:T(8,128)(2,1)} %copy-done.4), channel_id=1, source_target_pairs={{0,4},{4,0},{8,12},{12,8},{16,20},{20,16},{24,28},{28,24},{1,5},{5... | collective-permute-start | bytes 2654216 | tf_op jit(solution)/shard_map/ppermute | solution.py:69
  166.5 38.3 %collective-permute-start.3 = (bf16[256,1728]{0,1:T(8,128)(2,1)}, bf16[256,1728]{0,1:T(8,128)(2,1)}, u32[]{:S(2)}, u32[]{:S(2)}) collective-permute-start(bf16[256,1728]{0,1:T(8,128)(2,1)} %copy-done.10), channel_id=1, source_target_pairs={{0,4},{4,0},{8,12},{12,8},{16,20},{20,16},{24,28},{28,24},{1,5},{5... | collective-permute-start | bytes 2654216 | tf_op jit(solution)/shard_map/ppermute | solution.py:69
  208.9 223.4 %reduce-scatter.9.cloned.1.call-start = ((), (), s32[]{:S(2)}) async-start(), calls=%async_computation.7 | async-start | bytes 10321920 | tf_op jit(solution)/shard_map/reduce_scatter | solution.py:137
  212.3 26.0 %collective-permute-start.4 = (bf16[4,256,576]{1,2,0:T(8,128)(2,1)S(1)}, bf16[4,256,576]{1,2,0:T(8,128)(2,1)}, u32[]{:S(2)}, u32[]{:S(2)}) collective-permute-start(bf16[4,256,576]{1,2,0:T(8,128)(2,1)S(1)} %get-tuple-element.26), channel_id=1, source_target_pairs={{0,4},{4,0},{8,12},{12,8},{16,20},{20,16},{24,28},{28,24},{1,5},{5... | collective-permute-start | bytes 3538952 | tf_op jit(solution)/shard_map/ppermute | solution.py:69
  242.6 4.8 copy-start.3
  242.6 4.8 copy-start.7
  245.2 2.2 copy-start.1
  247.4 29.3 %copy-start.8 = (bf16[4,256,576]{1,2,0:T(8,128)(2,1)S(1)}, bf16[4,256,576]{1,2,0:T(8,128)(2,1)}, u32[]{:S(2)}) copy-start(bf16[4,256,576]{1,2,0:T(8,128)(2,1)} %get-tuple-element.14) | copy-start | bytes 3538948
  247.4 29.2 %copy-start.11 = (bf16[256,1728]{0,1:T(8,128)(2,1)S(1)}, bf16[256,1728]{0,1:T(8,128)(2,1)}, u32[]{:S(2)}) copy-start(bf16[256,1728]{0,1:T(8,128)(2,1)} %copy-done.10) | copy-start | bytes 2654212
  257.9 18.7 %collective-permute-start.5 = (bf16[256,1728]{0,1:T(8,128)(2,1)S(1)}, bf16[256,1728]{0,1:T(8,128)(2,1)S(1)}, u32[]{:S(2)}, u32[]{:S(2)}) collective-permute-start(bf16[256,1728]{0,1:T(8,128)(2,1)S(1)} %fusion.29), channel_id=1, source_target_pairs={{0,4},{4,0},{8,12},{12,8},{16,20},{20,16},{24,28},{28,24},{1,5},{5... | collective-permute-start | bytes 2654216 | tf_op jit(solution)/shard_map/ppermute | solution.py:69
  289.3 288.7 %reduce-scatter.11.cloned.1.call-start = ((), (), s32[]{:S(2)}) async-start(), calls=%async_computation.8 | async-start | bytes 10321920 | tf_op jit(solution)/shard_map/reduce_scatter | solution.py:137
  290.1 24.3 %copy-start.5 = (bf16[256,1728]{0,1:T(8,128)(2,1)S(1)}, bf16[256,1728]{0,1:T(8,128)(2,1)}, u32[]{:S(2)}) copy-start(bf16[256,1728]{0,1:T(8,128)(2,1)} %copy-done.4) | copy-start | bytes 2654212
  290.1 24.3 %copy-start.9 = (bf16[4,256,576]{1,2,0:T(8,128)(2,1)S(1)}, bf16[4,256,576]{1,2,0:T(8,128)(2,1)}, u32[]{:S(2)}) copy-start(bf16[4,256,576]{1,2,0:T(8,128)(2,1)} %get-tuple-element.20) | copy-start | bytes 3538948
  290.3 24.1 %collective-permute-start.6 = (bf16[4,256,576]{1,2,0:T(8,128)(2,1)S(1)}, bf16[4,256,576]{1,2,0:T(8,128)(2,1)S(1)}, u32[]{:S(2)}, u32[]{:S(2)}) collective-permute-start(bf16[4,256,576]{1,2,0:T(8,128)(2,1)S(1)} %get-tuple-element.25), channel_id=1, source_target_pairs={{0,4},{4,0},{8,12},{12,8},{16,20},{20,16},{24,28},{28,24},{1,5},{5... | collective-permute-start | bytes 3538952 | tf_op jit(solution)/shard_map/ppermute | solution.py:69
  (2 other events, 2.5 us)
Sparse Core Ops, SparseCore 0:
  10.1 24.2 all-gather.3
  59.7 33.0 reduce-scatter.12
  99.4 24.0 all-gather.5
  164.8 33.0 reduce-scatter.14
  209.1 24.0 all-gather.7
  289.4 142.9 reduce-scatter.8
  434.9 143.0 reduce-scatter.10

commit v3 on v2

--- a/solution.py
+++ b/solution.py
@@ -97,13 +97,38 @@
         other = lax.dynamic_index_in_dim(sets, 1 - low, 0, keepdims=False)
         return mine, to_partner(other)
 
+    alike = [[line * PAIR + part for line in range(lines)] for part in range(PAIR)]
+    line = group // PAIR
+
+    def gather_lines(factor):
+        return lax.all_gather(factor, "group", axis=0, axis_index_groups=alike, tiled=True)
+
+    def line_columns(factor):
+        weighted = (row_weight * factor.astype(jnp.float32)).astype(jnp.bfloat16)
+        sets = weighted.reshape(rows, lines, PAIR * block).transpose(1, 0, 2)
+        found = [lax.dynamic_index_in_dim(sets, line, 0, keepdims=False)]
+        for shift in range(1, lines):
+            moves = [
+                (at * PAIR + part, (at + shift) % lines * PAIR + part)
+                for at in range(lines)
+                for part in range(PAIR)
+            ]
+            leaving = lax.dynamic_index_in_dim(sets, (line + shift) % lines, 0, keepdims=False)
+            found.append(lax.ppermute(leaving, "group", moves))
+        return found
+
+    def in_line_order(found):
+        order = (line - jnp.arange(lines)) % lines
+        return jnp.stack(found)[order].reshape(lines * rows, PAIR * block)
+
     preact0 = contract_cols(inputs, up_weight)
     hidden0 = jax.nn.silu(preact0).astype(jnp.bfloat16)
     partial0 = jnp.dot(hidden0, down_weight, preferred_element_type=jnp.float32)
-    hidden0_far = to_partner(hidden0)
     input_grams = gram(inputs, inputs, clients)
     input_cols = column_sets(inputs)
-    residual0, hidden0_far, input_cols = residual_of(partial0, hidden0_far, input_cols)
+    residual0, _, input_cols = residual_of(partial0, (), input_cols)
+    residual0, hidden0 = lax.optimization_barrier((residual0, hidden0))
+    hidden0_all = gather_lines(hidden0)
     slopes0 = (contract_cols(residual0, down_weight) * silu_slope(preact0)).astype(jnp.bfloat16)
     slopes0_far = to_partner(slopes0)
 
@@ -112,44 +137,44 @@
     partial1 = jnp.dot(
         hidden1, down_weight, preferred_element_type=jnp.float32
     ) - correction(gram(hidden1, hidden0, clients), residual0, clients)
-    hidden1_far = to_partner(hidden1)
-    residual0_cols = column_sets(residual0)
-    residual1, (hidden1_far, slopes0_far), residual0_cols = residual_of(
-        partial1, (hidden1_far, slopes0_far), residual0_cols
-    )
-    residual1_cols = column_sets(residual1)
+    residual0_cols = line_columns(residual0)
+    residual1, hidden0_all, (slopes0_far, residual0_cols) = residual_of(
+        partial1, hidden0_all, (slopes0_far, residual0_cols)
+    )
+    residual1, hidden1 = lax.optimization_barrier((residual1, hidden1))
+    hidden1_all = gather_lines(hidden1)
+    residual1_cols = line_columns(residual1)
     back1 = contract_cols(residual1, down_weight) - correction(
         gram(residual1, residual0, clients), hidden0, clients
     )
     slopes1 = (back1 * silu_slope(preact1)).astype(jnp.bfloat16)
     slopes1_far = to_partner(slopes1)
+    slopes1_far, hidden1_all = lax.optimization_barrier((slopes1_far, hidden1_all))
 
     weight_total = jnp.sum(sample_counts).astype(jnp.float32)
-    alike = [[line * PAIR + part for line in range(lines)] for part in range(PAIR)]
-
-    def server_sum(left, right):
-        pair_sum = jnp.einsum(
-            "nkc,kf->ncf",
-            jnp.concatenate(right, axis=1),
-            jnp.concatenate(left, axis=0),
-            preferred_element_type=jnp.float32,
-        ).astype(jnp.bfloat16)
-        return lax.psum_scatter(
-            pair_sum.reshape(lines * block, hidden_count),
-            "group",
-            scatter_dimension=0,
-            axis_index_groups=alike,
-            tiled=True,
-        ).T.astype(jnp.float32)
-
-    sum_down = server_sum(
-        (hidden0, hidden1, hidden0_far, hidden1_far),
-        (residual0_cols[0], residual1_cols[0], residual0_cols[1], residual1_cols[1]),
-    )
-    sum_up = server_sum(
-        (slopes0, slopes1, slopes0_far, slopes1_far),
-        (input_cols[0], input_cols[0], input_cols[1], input_cols[1]),
-    )
+
+    pair_sum = jnp.einsum(
+        "nkc,kf->ncf",
+        jnp.concatenate((input_cols[0], input_cols[0], input_cols[1], input_cols[1]), axis=1),
+        jnp.concatenate((slopes0, slopes1, slopes0_far, slopes1_far), axis=0),
+        preferred_element_type=jnp.float32,
+    ).astype(jnp.bfloat16)
+    sum_up = lax.psum_scatter(
+        pair_sum.reshape(lines * block, hidden_count),
+        "group",
+        scatter_dimension=0,
+        axis_index_groups=alike,
+        tiled=True,
+    ).T.astype(jnp.float32)
+
+    line_hidden = jnp.concatenate((hidden0_all, hidden1_all), axis=0)
+    line_cols = jnp.concatenate((in_line_order(residual0_cols), in_line_order(residual1_cols)))
+    line_sum = jnp.einsum(
+        "kc,kf->cf", line_cols, line_hidden, preferred_element_type=jnp.float32
+    ).astype(jnp.bfloat16).reshape(PAIR, block, hidden_count)
+    kept = lax.dynamic_index_in_dim(line_sum, low, 0, keepdims=False)
+    came = to_partner(lax.dynamic_index_in_dim(line_sum, 1 - low, 0, keepdims=False))
+    sum_down = (kept.astype(jnp.float32) + came.astype(jnp.float32)).T
     new_momentum_up = momentum_decay * momentum_up + sum_up / weight_total
     new_momentum_down = momentum_decay * momentum_down + sum_down / weight_total
     return (new_momentum_up, new_momentum_down)

time: 600 us -> 642 us (1.070)
  local copies, waits for them, and re-layouts: 31.8 us -> 58.7 us
  starting transfers between devices: 10.5 us -> 17.3 us
    reduce_scatter x2 -> x1, waiting for transfers between devices: 244 us -> 0.01 us  [on_device(): lax.psum_scatter(pair_sum.reshape(lines * block, hidden_count), 'group',...]
    ppermute x0 -> x6, waiting for transfers between devices: none -> 157 us  [line_columns(): found.append(lax.ppermute(leaving, 'group', moves))]
    all_gather x0 -> x2, waiting for transfers between devices: none -> 90.6 us  [gather_lines(): lax.all_gather(factor, 'group', axis=0, axis_index_groups=alike, tiled=True)]
    unnamed x42 -> x41, local copies, waits for them, and re-layouts: 7.68 us -> 23 us
    ppermute x0 -> x6, starting transfers between devices: none -> 11.6 us  [line_columns(): found.append(lax.ppermute(leaving, 'group', moves))]
    ppermute x7 -> x4, waiting for transfers between devices: 91.4 us -> 87.6 us  [to_partner(): return lax.ppermute(array, 'group', across)]
    unnamed x9 -> x10, waiting for transfers between devices: 62 us -> 64.6 us
  transfers between devices with their start and end apart: 14 -> 18, of which waited for: 10 -> 14; matrix products, arithmetic and copies ran while one was open for 6% -> 12% of each run, Pallas kernels for 0% -> 0%
where the time goes in v3:
time: 642 us; the launch traced here: 634 us
  waiting for transfers between devices  425 us (66%)
  matrix products  94.1 us (15%)
  local copies, waits for them, and re-layouts  58.7 us (9%)
  other arithmetic  24.1 us (4%)
  starting transfers between devices  17.3 us (3%)
  between operations  15.6 us (2%)
    ppermute x6, waiting for transfers between devices, line_columns(): found.append(lax.ppermute(leaving, 'group', moves))  157 us
    all_gather x2, waiting for transfers between devices, gather_lines(): lax.all_gather(factor, 'group', axis=0, axis_index_groups=alike, tiled=True)  90.6 us
    ppermute x4, waiting for transfers between devices, to_partner(): return lax.ppermute(array, 'group', across)  87.6 us
    unnamed x10, waiting for transfers between devices  64.6 us
    dot_general x3, matrix products, contract_cols(): lax.dot_general(former, latter, (((1,), (1,)), ((), ())), preferred_eleme...  34 us
    all_gather x3, waiting for transfers between devices, gather_cols(): return lax.all_gather(array, 'tensor', axis=1, tiled=True)  25.1 us
    unnamed x41, local copies, waits for them, and re-layouts  23 us
    dot_general x1, matrix products, on_device(): jnp.einsum('kc,kf->cf', line_cols, line_hidden, preferred_element_type=jn...  14.4 us
  transfers between devices with their start and end apart: 18, of which 14 were waited for; matrix products, arithmetic and copies ran while one was open for 12% of the time, Pallas kernels for 0%

profile of v3, /device:TPU:10, one launch (start us, length us, event | category | flops | bytes accessed | tf_op | source)
XLA Modules:
  0.0 634.4 jit_solution(12400588981015251444)
XLA Ops:
  9.4 25.1 %all-gather.6.cloned.1.call-done = bf16[256,4608]{0,1:T(8,128)(2,1)} async-done(((bf16[256,1152]{0,1:T(8,128)(2,1)}), bf16[256,4608]{0,1:T(8,128)(2,1)}) %all-gather.6.cloned.1.call-update) | async-done | bytes 2359312 | tf_op jit(solution)/shard_map/all_gather | solution.py:72
  34.5 12.0 %multiply_convert_fusion.4 = (bf16[256,1728]{0,1:T(8,128)(2,1)S(1)}, f32[256,1728]{0,1:T(8,128)}) fusion(bf16[1728,4608]{1,0:T(8,128)(2,1)} %param.12, bf16[256,4608]{0,1:T(8,128)(2,1)} %all-gather.6.cloned.1.call-done), kind=kOutput, calls=%fused_computation.46 | convolution fusion | flops 4079075328 | bytes 20938752 | tf_op jit(solution)/shard_map/dot_general | solution.py:19
  46.5 10.6 %convolution_convert_fusion.1 = bf16[256,4608]{1,0:T(8,128)(2,1)S(1)} fusion(bf16[256,1728]{0,1:T(8,128)(2,1)S(1)} %get-tuple-element.23, bf16[1728,4608]{1,0:T(8,128)(2,1)} %param.13), kind=kOutput, calls=%fused_computation.8 | convolution fusion | flops 4078043136 | bytes 19169280 | tf_op jit(solution)/shard_map/dot_general | solution.py:126
  61.2 31.6 %reduce-scatter.10.cloned.1.call-done = bf16[1152,256]{1,0:T(8,128)(2,1)} async-done(((bf16[4608,256]{1,0:T(8,128)(2,1)}), bf16[1152,256]{1,0:T(8,128)(2,1)}) %reduce-scatter.10.cloned.1.call-update) | async-done | bytes 589840
  103.1 2.8 copy.39
  107.4 22.3 %collective-permute-done = bf16[4,256,576]{1,2,0:T(8,128)(2,1)} collective-permute-done((bf16[4,256,576]{1,2,0:T(8,128)(2,1)}, bf16[4,256,576]{1,2,0:T(8,128)(2,1)}, u32[]{:S(2)}, u32[]{:S(2)}) %collective-permute-start) | collective-permute-done | bytes 1179680 | tf_op jit(solution)/shard_map/ppermute | solution.py:69
  129.7 2.8 copy.66
  132.6 11.5 %fusion.24 = bf16[256,1728]{0,1:T(8,128)(2,1)S(1)} fusion(bf16[1728,4608]{1,0:T(8,128)(2,1)} %param.13, bf16[256,4608]{0,1:T(8,128)(2,1)} %all-gather.8.cloned.1.call-done, f32[256,1728]{0,1:T(8,128)} %get-tuple-element.47), kind=kOutput, calls=%fused_computation.38 | convolution fusion | flops 4080844800 | bytes 20938752 | tf_op jit(solution)/shard_map/dot_general | solution.py:19
  152.6 11.5 %fusion.3 = bf16[256,4608]{1,0:T(8,128)(2,1)} fusion(f32[256,4608]{1,0:T(8,128)S(1)} %bitcast.125, bf16[256,1728]{0,1:T(8,128)(2,1)S(1)} %copy-done.4, bf16[1728,4608]{1,0:T(8,128)(2,1)} %param.13), kind=kOutput, calls=%fused_computation.7 | convolution fusion | flops 4079222784 | bytes 23887872 | tf_op jit(solution)/shard_map/dot_general | solution.py:137
  164.1 4.3 copy.64
  169.3 32.4 %reduce-scatter.12.cloned.1.call-done = bf16[1152,256]{1,0:T(8,128)(2,1)} async-done(((bf16[4608,256]{1,0:T(8,128)(2,1)}), bf16[1152,256]{1,0:T(8,128)(2,1)}) %reduce-scatter.12.cloned.1.call-update) | async-done | bytes 589840
  203.7 67.3 %all-gather.10.cloned.1.call-done = bf16[1024,1728]{0,1:T(8,128)(2,1)} async-done(((bf16[256,1728]{0,1:T(8,128)(2,1)}), bf16[1024,1728]{0,1:T(8,128)(2,1)}) %all-gather.10.cloned.1.call-update) | async-done | bytes 3538960 | tf_op jit(solution)/shard_map/all_gather | solution.py:104
  286.9 3.2 collective-permute-start.3
  291.5 32.5 %collective-permute-done.2 = bf16[256,1152]{1,0:T(8,128)(2,1)} collective-permute-done((bf16[256,1152]{1,0:T(8,128)(2,1)}, bf16[256,1152]{1,0:T(8,128)(2,1)}, u32[]{:S(2)}, u32[]{:S(2)}) %collective-permute-start.2) | collective-permute-done | bytes 589856 | tf_op jit(solution)/shard_map/ppermute | solution.py:117
  324.0 11.3 %collective-permute-done.3 = bf16[256,1152]{1,0:T(8,128)(2,1)} collective-permute-done((bf16[256,1152]{1,0:T(8,128)(2,1)}, bf16[256,1152]{1,0:T(8,128)(2,1)}, u32[]{:S(2)}, u32[]{:S(2)}) %collective-permute-start.3) | collective-permute-done | bytes 589856 | tf_op jit(solution)/shard_map/ppermute | solution.py:117
  335.3 4.0 collective-permute-done.4
  339.4 4.3 copy.61
  343.6 2.8 convolution_multiply_fusion.1
  348.3 10.5 %fusion.25 = bf16[256,1728]{0,1:T(8,128)(2,1)S(1)} fusion(bf16[1728,4608]{1,0:T(8,128)(2,1)} %param.13, bf16[256,4608]{0,1:T(8,128)(2,1)S(1)} %copy-done, f32[2,216,8,128]{3,2,1,0:T(8,128)S(1)} %convolution_bitcast_fusion, f32[256,1728]{0,1:T(8,128)S(1)} %copy-done.8, f32[2,216,8,128]{3,2,1,0:T(8,128)S(1)} %copy-done.6), kind=kOutput, calls=%fused_computation.39 | convolution fusion | flops 4081729536 | bytes 24477696 | tf_op jit(solution)/shard_map/dot_general | solution.py:19
  360.3 21.1 %collective-permute-done.5 = bf16[256,1728]{0,1:T(8,128)(2,1)} collective-permute-done((bf16[256,1728]{0,1:T(8,128)(2,1)S(1)}, bf16[256,1728]{0,1:T(8,128)(2,1)}, u32[]{:S(2)}, u32[]{:S(2)}) %collective-permute-start.5) | collective-permute-done | bytes 884768 | tf_op jit(solution)/shard_map/ppermute | solution.py:69
  381.4 23.3 %all-gather.14.cloned.1.call-done = bf16[1024,1728]{0,1:T(8,128)(2,1)} async-done(((bf16[256,1728]{0,1:T(8,128)(2,1)}), bf16[1024,1728]{0,1:T(8,128)(2,1)}) %all-gather.14.cloned.1.call-update) | async-done | bytes 3538960 | tf_op jit(solution)/shard_map/all_gather | solution.py:104
  404.7 13.6 %convolution_convert_fusion.2 = bf16[4,576,1728]{2,1,0:T(8,128)(2,1)} fusion(bf16[4,256,576]{1,2,0:T(8,128)(2,1)} %collective-permute-done, bf16[4,256,576]{1,2,0:T(8,128)(2,1)} %get-tuple-element.19, bf16[256,1728]{0,1:T(8,128)(2,1)} %collective-permute-done.5, bf16[256,1728]{0,1:T(8,128)(2,1)} %collective-permute-done.1, bf16[256,1728]{0,1:T(8,128)(2,1)} %copy-done.12, ...), kind=kOutput, calls=%fused_computation.9 | convolution fusion | flops 8190738432 | bytes 13860864 | tf_op jit(solution)/shard_map/nkc,kf->ncf/dot_general | solution.py:156
  423.6 3.2 collective-permute-start.7
  432.4 31.0 %collective-permute-done.6 = bf16[256,1152]{1,0:T(8,128)(2,1)} collective-permute-done((bf16[256,1152]{1,0:T(8,128)(2,1)}, bf16[256,1152]{1,0:T(8,128)(2,1)}, u32[]{:S(2)}, u32[]{:S(2)}) %collective-permute-start.6) | collective-permute-done | bytes 589856 | tf_op jit(solution)/shard_map/ppermute | solution.py:117
  463.4 66.5 %collective-permute-done.7 = bf16[256,1152]{1,0:T(8,128)(2,1)} collective-permute-done((bf16[256,1152]{1,0:T(8,128)(2,1)}, bf16[256,1152]{1,0:T(8,128)(2,1)}, u32[]{:S(2)}, u32[]{:S(2)}) %collective-permute-start.7) | collective-permute-done | bytes 589856 | tf_op jit(solution)/shard_map/ppermute | solution.py:117
  530.0 11.3 %collective-permute-done.8 = bf16[256,1152]{1,0:T(8,128)(2,1)} collective-permute-done((bf16[256,1152]{1,0:T(8,128)(2,1)}, bf16[256,1152]{1,0:T(8,128)(2,1)}, u32[]{:S(2)}, u32[]{:S(2)}) %collective-permute-start.8) | collective-permute-done | bytes 589856 | tf_op jit(solution)/shard_map/ppermute | solution.py:117
  545.4 14.4 %convolution_convert_fusion = bf16[1152,1728]{0,1:T(8,128)(2,1)} fusion(bf16[1024,1728]{0,1:T(8,128)(2,1)} %all-gather.14.cloned.1.call-done, bf16[1024,1728]{0,1:T(8,128)(2,1)} %all-gather.10.cloned.1.call-done, bf16[1024,1152]{1,0:T(8,128)(2,1)} %bitcast.138, bf16[1024,1152]{1,0:T(8,128)(2,1)} %bitcast.137), kind=kOutput, calls=%fused_computation.2 | convolution fusion | flops 8179310592 | bytes 15777792 | tf_op jit(solution)/shard_map/kc,kf->cf/dot_general | solution.py:172
  559.8 6.4 %copy.58 = bf16[1152,1728]{1,0:T(8,128)(2,1)} copy(bf16[1152,1728]{0,1:T(8,128)(2,1)} %convolution_convert_fusion) | data formatting | bytes 7962624 | tf_op jit(solution)/shard_map/convert_element_type | solution.py:174
  566.2 3.0 dynamic-slice_bitcast_fusion
  572.0 44.2 %collective-permute-done.9 = bf16[576,1728]{1,0:T(8,128)(2,1)S(1)} collective-permute-done((bf16[576,1728]{1,0:T(8,128)(2,1)}, bf16[576,1728]{1,0:T(8,128)(2,1)S(1)}, u32[]{:S(2)}, u32[]{:S(2)}) %collective-permute-start.9) | collective-permute-done | bytes 1990688 | tf_op jit(solution)/shard_map/ppermute | solution.py:69
  616.2 5.6 fusion.16
  621.8 5.3 bitcast_add_fusion
  (98 shorter events, 67.0 us)
Async XLA Ops:
  7.2 27.3 %all-gather.6.cloned.1.call-start = ((), (), s32[]{:S(2)}) async-start(), calls=%async_computation.3 | async-start | bytes 2949120 | tf_op jit(solution)/shard_map/all_gather | solution.py:72
  9.4 83.4 %reduce-scatter.10.cloned.1.call-start = ((), (), s32[]{:S(2)}) async-start(), calls=%async_computation.9 | async-start | bytes 2949120
  46.5 10.6 %copy-start.2 = (bf16[256,1728]{0,1:T(8,128)(2,1)}, bf16[256,1728]{0,1:T(8,128)(2,1)S(1)}, u32[]{:S(2)}) copy-start(bf16[256,1728]{0,1:T(8,128)(2,1)S(1)} %get-tuple-element.23) | copy-start | bytes 2654212
  59.5 1.1 copy-start.10
  59.5 1.5 copy-start.13
  59.6 70.2 %all-gather.8.cloned.1.call-start = ((), (), s32[]{:S(2)}) async-start(), calls=%async_computation.4 | async-start | bytes 2949120 | tf_op jit(solution)/shard_map/all_gather | solution.py:72
  94.9 4.6 copy-start.14
  94.9 4.7 copy-start.1
  99.2 102.4 %reduce-scatter.12.cloned.1.call-start = ((), (), s32[]{:S(2)}) async-start(), calls=%async_computation.10 | async-start | bytes 2949120
  101.7 28.0 %collective-permute-start = (bf16[4,256,576]{1,2,0:T(8,128)(2,1)}, bf16[4,256,576]{1,2,0:T(8,128)(2,1)}, u32[]{:S(2)}, u32[]{:S(2)}) collective-permute-start(bf16[4,256,576]{1,2,0:T(8,128)(2,1)} %get-tuple-element.44), channel_id=1, source_target_pairs={{0,4},{4,0},{8,12},{12,8},{16,20},{20,16},{24,28},{28,24},{1,5},{5... | collective-permute-start | bytes 3538952 | tf_op jit(solution)/shard_map/ppermute | solution.py:69
  132.5 12.5 %copy-start.11 = (f32[2,128,128]{2,1,0:T(8,128)S(1)}, f32[2,128,128]{2,1,0:T(8,128)}, u32[]{:S(2)}) copy-start(f32[2,128,128]{2,1,0:T(8,128)} %convolution_multiply_fusion.2) | copy-start | bytes 393220
  144.0 1.0 copy-start.9
  145.0 2.1 copy-start.7
  145.9 1.2 copy-start.5
  150.5 2.1 copy-start.4
  168.4 102.7 %all-gather.10.cloned.1.call-start = ((), (), s32[]{:S(2)}) async-start(), calls=%async_computation.5 | async-start | bytes 4423680 | tf_op jit(solution)/shard_map/all_gather | solution.py:104
  169.0 170.3 %all-gather.12.cloned.1.call-start = ((), (), s32[]{:S(2)}) async-start(), calls=%async_computation.6 | async-start | bytes 2949120 | tf_op jit(solution)/shard_map/all_gather | solution.py:72
  275.2 129.5 %all-gather.14.cloned.1.call-start = ((), (), s32[]{:S(2)}) async-start(), calls=%async_computation.7 | async-start | bytes 4423680 | tf_op jit(solution)/shard_map/all_gather | solution.py:104
  275.4 63.9 %collective-permute-start.1 = (bf16[256,1728]{0,1:T(8,128)(2,1)}, bf16[256,1728]{0,1:T(8,128)(2,1)}, u32[]{:S(2)}, u32[]{:S(2)}) collective-permute-start(bf16[256,1728]{0,1:T(8,128)(2,1)} %copy-done.9), channel_id=1, source_target_pairs={{0,4},{4,0},{8,12},{12,8},{16,20},{20,16},{24,28},{28,24},{1,5},{5... | collective-permute-start | bytes 2654216 | tf_op jit(solution)/shard_map/ppermute | solution.py:69
  282.3 41.7 %collective-permute-start.2 = (bf16[256,1152]{1,0:T(8,128)(2,1)}, bf16[256,1152]{1,0:T(8,128)(2,1)}, u32[]{:S(2)}, u32[]{:S(2)}) collective-permute-start(bf16[256,1152]{1,0:T(8,128)(2,1)} %bitcast.140), channel_id=1, source_target_pairs={{0,8},{4,12},{8,16},{12,20},{16,24},{20,28},{24,0},{28,4},{1,9},{5... | collective-permute-start | bytes 1769480 | tf_op jit(solution)/shard_map/ppermute | solution.py:117
  286.9 48.4 %collective-permute-start.3 = (bf16[256,1152]{1,0:T(8,128)(2,1)}, bf16[256,1152]{1,0:T(8,128)(2,1)}, u32[]{:S(2)}, u32[]{:S(2)}) collective-permute-start(bf16[256,1152]{1,0:T(8,128)(2,1)} %bitcast.142), channel_id=1, source_target_pairs={{0,16},{4,20},{8,24},{12,28},{16,0},{20,4},{24,8},{28,12},{1,17},{... | collective-permute-start | bytes 1769480 | tf_op jit(solution)/shard_map/ppermute | solution.py:117
  291.2 48.1 %collective-permute-start.4 = (bf16[256,1152]{1,0:T(8,128)(2,1)}, bf16[256,1152]{1,0:T(8,128)(2,1)}, u32[]{:S(2)}, u32[]{:S(2)}) collective-permute-start(bf16[256,1152]{1,0:T(8,128)(2,1)} %bitcast.143), channel_id=1, source_target_pairs={{0,24},{4,28},{8,0},{12,4},{16,8},{20,12},{24,16},{28,20},{1,25},{... | collective-permute-start | bytes 1769480 | tf_op jit(solution)/shard_map/ppermute | solution.py:117
  339.3 282.5 %reduce-scatter.8.cloned.1.call-start = ((), (), s32[]{:S(2)}) async-start(), calls=%async_computation.8 | async-start | bytes 10321920 | tf_op jit(solution)/shard_map/reduce_scatter | solution.py:162
  343.6 2.8 copy-start.3
  343.6 3.7 copy-start.6
  343.6 3.7 copy-start.8
  346.4 1.9 copy-start
  359.8 21.7 %collective-permute-start.5 = (bf16[256,1728]{0,1:T(8,128)(2,1)S(1)}, bf16[256,1728]{0,1:T(8,128)(2,1)}, u32[]{:S(2)}, u32[]{:S(2)}) collective-permute-start(bf16[256,1728]{0,1:T(8,128)(2,1)S(1)} %fusion.25), channel_id=1, source_target_pairs={{0,4},{4,0},{8,12},{12,8},{16,20},{20,16},{24,28},{28,24},{1,5},{5... | collective-permute-start | bytes 2654216 | tf_op jit(solution)/shard_map/ppermute | solution.py:69
  420.1 43.4 %collective-permute-start.6 = (bf16[256,1152]{1,0:T(8,128)(2,1)}, bf16[256,1152]{1,0:T(8,128)(2,1)}, u32[]{:S(2)}, u32[]{:S(2)}) collective-permute-start(bf16[256,1152]{1,0:T(8,128)(2,1)} %bitcast.29), channel_id=1, source_target_pairs={{0,8},{4,12},{8,16},{12,20},{16,24},{20,28},{24,0},{28,4},{1,9},{5... | collective-permute-start | bytes 1769480 | tf_op jit(solution)/shard_map/ppermute | solution.py:117
  423.6 106.4 %collective-permute-start.7 = (bf16[256,1152]{1,0:T(8,128)(2,1)}, bf16[256,1152]{1,0:T(8,128)(2,1)}, u32[]{:S(2)}, u32[]{:S(2)}) collective-permute-start(bf16[256,1152]{1,0:T(8,128)(2,1)} %bitcast.31), channel_id=1, source_target_pairs={{0,16},{4,20},{8,24},{12,28},{16,0},{20,4},{24,8},{28,12},{1,17},{... | collective-permute-start | bytes 1769480 | tf_op jit(solution)/shard_map/ppermute | solution.py:117
  427.8 113.4 %collective-permute-start.8 = (bf16[256,1152]{1,0:T(8,128)(2,1)}, bf16[256,1152]{1,0:T(8,128)(2,1)}, u32[]{:S(2)}, u32[]{:S(2)}) collective-permute-start(bf16[256,1152]{1,0:T(8,128)(2,1)} %bitcast.33), channel_id=1, source_target_pairs={{0,24},{4,28},{8,0},{12,4},{16,8},{20,12},{24,16},{28,20},{1,25},{... | collective-permute-start | bytes 1769480 | tf_op jit(solution)/shard_map/ppermute | solution.py:117
  569.2 47.0 %collective-permute-start.9 = (bf16[576,1728]{1,0:T(8,128)(2,1)}, bf16[576,1728]{1,0:T(8,128)(2,1)S(1)}, u32[]{:S(2)}, u32[]{:S(2)}) collective-permute-start(bf16[576,1728]{1,0:T(8,128)(2,1)} %dynamic-slice_bitcast_fusion), channel_id=1, source_target_pairs={{0,4},{4,0},{8,12},{12,8},{16,20},{20,16},{24,28},{28,24},{1,5},{5... | collective-permute-start | bytes 5971976 | tf_op jit(solution)/shard_map/ppermute | solution.py:69
  (1 other events, 0.9 us)
Sparse Core Ops, SparseCore 0:
  10.1 24.2 all-gather.5
  59.7 33.0 reduce-scatter.9
  99.3 24.0 all-gather.7
  168.5 33.0 reduce-scatter.11
  203.0 68.0 all-gather.9
  275.4 24.0 all-gather.11
  339.4 65.2 all-gather.13
  418.5 192.6 reduce-scatter.7
